TPU v7x, 256 devices: a whole 4x4x8 slice. The times are simulated.
256 devices in a mesh: pipe: 16 (over z_lo, x, core), tp: 16 (over y, z_hi).
Axes of the slice: x: 4, y: 4, z: 8 (z_hi: 4, z_lo: 2; z = z_hi * 2 + z_lo), core: 2. Of those that a mesh axis runs over, the one named last changes fastest.
Arguments:
- x_fwd: bfloat16 [16, 256, 6144], P('pipe', None, 'tp'), may hold values from -6 to 6
- cotangent: bfloat16 [16, 256, 6144], P('pipe', None, 'tp'), may hold values from -6 to 6
- ln_gain: bfloat16 [16, 6144], P('pipe', 'tp'), may hold values from 0.5 to 2
- ln_bias: bfloat16 [16, 6144], P('pipe', 'tp'), may hold values from -3 to 3
- w_value: bfloat16 [16, 6144, 6144], P('pipe', None, 'tp'), may hold values from -1 to 1
- w_out: bfloat16 [16, 6144, 6144], P('pipe', 'tp'), may hold values from -0.15625 to 0.15625
- scores_fwd: float32 [16, 48, 256, 256], P('pipe', 'tp'), may hold values from -9 to 400, as said below
- scores_bwd: float32 [16, 48, 256, 256], P('pipe', 'tp'), may hold values from -9 to 400, as said below
- stash_codes: bfloat16 [16, 256, 6144], P('pipe', None, 'tp'), may hold values from -448 to 448
- stash_scales: bfloat16 [16, 48, 256], P('pipe', 'tp'), may hold values from 0.005 to 0.151
- evict: int32 [16, 256], P('pipe'), may hold values from 0 to 15, as said below
Outputs:
- fwd_next: bfloat16 [16, 256, 6144], P('pipe', None, 'tp')
- bwd_next: bfloat16 [16, 256, 6144], P('pipe', None, 'tp')
Inputs may be any that keep to these rules, and one draw needn't show every extreme that they name: `scores_fwd`: pre-softmax scores. `scores_bwd`: pre-softmax scores. evict[s, t] is s or 15 - s, and evict[evict[s, t], t] = s; every token of section 0 has its stash held by section 15.
All inputs are finite; a program needn't handle non-finite values.
Results may differ from a plain program's by a relative error of at most 0.017.
Values may be sent and summed in bfloat16 or wider, within the bound.
No kernel may reach another device: no remote copies, remote signals or barrier semaphores. Data moves between devices by JAX's collectives and lax.ppermute only.
A program may use at most 64 MiB of HBM per device.

v0:
```python
import jax
import jax.numpy as jnp
from jax import lax
from jax.experimental import pallas as pl
from jax.experimental.pallas import tpu as pltpu
from jax.sharding import Mesh, PartitionSpec as P

norm_epsilon = 1e-05
SIDE = 4
F32 = jnp.float32
BF16 = jnp.bfloat16
NT = (((1,), (1,)), ((), ()))
NN = (((1,), (0,)), ((), ()))
VMEM_LIMIT = 56 * 1024 * 1024


def turned(value, axis, steps):
    return lax.ppermute(value, axis, [(i, (i + steps) % SIDE) for i in range(SIDE)])


def shifted(value, axis, steps):
    count = lax.axis_size(axis)
    first, last = (max(0, -steps), min(count, count - steps))
    return lax.ppermute(value, axis, [(source, source + steps) for source in range(first, last)])


def shifted_turned(value, steps):
    count = lax.axis_size("pipe")
    pairs = [
        (s * SIDE + i, (s + 1) * SIDE + (i + steps) % SIDE)
        for s in range(count - 1)
        for i in range(SIDE)
    ]
    return lax.ppermute(value, ("pipe", "z"), pairs)


def mirrored(value):
    count = lax.axis_size("pipe")
    return lax.ppermute(value, "pipe", [(s, count - 1 - s) for s in range(count)])


def add(left, right):
    return (left.astype(F32) + right.astype(F32)).astype(BF16)


def weights_kernel(fwd_ref, bwd_ref, fwd_out, bwd_out):
    size = fwd_ref.shape[-1]
    query = lax.broadcasted_iota(jnp.int32, (size, size), 0)
    key = lax.broadcasted_iota(jnp.int32, (size, size), 1)

    def causal(scores):
        masked = jnp.where(key <= query, scores, -jnp.inf)
        raised = jnp.exp(masked - jnp.max(masked, axis=-1, keepdims=True))
        return raised / jnp.sum(raised, axis=-1, keepdims=True)

    for head in range(fwd_ref.shape[0]):
        bwd_out[head] = causal(bwd_ref[head]).T.astype(BF16)
        fwd_out[head] = causal(fwd_ref[head]).astype(BF16)


ORDER = [4, 5, 3, 6, 2, 7, 0, 1]


def start_weights(place, wv_hbm, wo_hbm, wv, wo, sem_v, sem_o, value_first):
    width = wv_hbm.shape[1]

    def copies(j, second):
        relative = second or (value_first and j // SIDE == 2)
        k = lax.rem(place[1] + j % SIDE, SIDE) if relative else j % SIDE
        block = lax.rem(place[0] + j // SIDE, SIDE) * SIDE + k
        at = pl.ds(pl.multiple_of(block * width, 128), width)
        here = slice(j * width, (j + 1) * width)
        if second != value_first:
            return pltpu.make_async_copy(wv_hbm.at[at, :], wv.at[here, :], sem_v.at[j])
        return pltpu.make_async_copy(wo_hbm.at[:, at], wo.at[:, here], sem_o.at[j])

    first = [copies(j, False) for j in range(SIDE * SIDE)]
    second = [copies(j, True) for j in range(SIDE * SIDE)]
    for c in first:
        c.start()
    for pair in ORDER:
        second[2 * pair].start()
        second[2 * pair + 1].start()
    return first, second


def start_pieces(refs, held, sem):
    near, right, left, far_a, far_b = refs
    two, three = pl.ds(0, 2), pl.ds(0, 3)
    if len(far_a.shape) == 2:
        far = [(far_a, held.at[8]), (far_b.at[three], held.at[pl.ds(9, 3)])]
    else:
        far = [(far_a.at[two], held.at[pl.ds(8, 2)]), (far_b.at[two], held.at[pl.ds(10, 2)])]
    moves = [
        (near, held.at[pl.ds(0, 4)]),
        (right, held.at[pl.ds(4, 4)]),
        *far,
        (left, held.at[pl.ds(12, 4)]),
    ]
    copies = [pltpu.make_async_copy(*move, sem.at[i]) for i, move in enumerate(moves)]
    for c in copies:
        c.start()
    return [copies[0:1], [], copies[1:2], [], copies[2:4], [], copies[4:5], []]


def give_parts(product, refs, parts, sem, width):
    p2a, p2b, p1, p3, p0 = refs
    outs = [(p0, 0), (p0, 2), (p1, 0), (p1, 2), (p2a, 0), (p2b, 0), (p3, 0), (p3, 2)]
    copies = []
    for pair in ORDER:
        ref, at = outs[pair]
        wide = product(pair).astype(BF16)
        parts[2 * pair] = wide[:, :width]
        parts[2 * pair + 1] = wide[:, width:]
        copies.append(
            pltpu.make_async_copy(
                parts.at[pl.ds(2 * pair, 2)], ref.at[pl.ds(at, 2)], sem.at[pair]
            )
        )
        copies[-1].start()
    for c in copies:
        c.wait()


def mix(weights, values):
    size = values.shape[1] // weights.shape[0]
    heads = [
        lax.dot_general(
            weights[h], values[:, h * size : (h + 1) * size], NN, preferred_element_type=F32
        ).astype(BF16)
        for h in range(weights.shape[0])
    ]
    return jnp.concatenate(heads, axis=1)


def bwd_kernel(
    place, near, right, left, fa, fb, weights, wv_hbm, wo_hbm,
    p2a, p2b, p1, p3, p0,
    held, parts, wv, wo, sem_in, sem_out, sem_v, sem_o,
):
    rows, width = parts.shape[1:]
    arriving = start_pieces((near, right, left, fa, fb), held, sem_in)
    out, value = start_weights(place, wv_hbm, wo_hbm, wv, wo, sem_v, sem_o, False)
    total = jnp.zeros((rows, width), F32)
    for pair in range(SIDE * SIDE // 2):
        for c in arriving[pair]:
            c.wait()
        out[2 * pair].wait()
        out[2 * pair + 1].wait()
        wide = jnp.concatenate([held[2 * pair], held[2 * pair + 1]], axis=1)
        total += lax.dot_general(
            wide, wo[:, 2 * pair * width : 2 * (pair + 1) * width], NT, preferred_element_type=F32
        )
    grads = mix(weights, total.astype(BF16))

    def product(pair):
        value[2 * pair].wait()
        value[2 * pair + 1].wait()
        return lax.dot_general(
            grads, wv[2 * pair * width : 2 * (pair + 1) * width, :], NT, preferred_element_type=F32
        )

    give_parts(product, (p2a, p2b, p1, p3, p0), parts, sem_out, width)


def fwd_kernel(
    place, near, right, left, fa, fb, weights, wv_hbm, wo_hbm,
    p2a, p2b, p1, p3, p0,
    held, parts, wv, wo, sem_in, sem_out, sem_v, sem_o,
):
    rows, width = parts.shape[1:]
    arriving = start_pieces((near, right, left, fa, fb), held, sem_in)
    value, out = start_weights(place, wv_hbm, wo_hbm, wv, wo, sem_v, sem_o, True)
    full = width * SIDE * SIDE
    sums = jnp.zeros((rows, 128), F32)
    squares = jnp.zeros((rows, 128), F32)
    for one in range(SIDE * SIDE):
        if one % 2 == 0:
            for c in arriving[one // 2]:
                c.wait()
        for c in range(0, width, 128):
            part = held[one, :rows, c : c + 128].astype(F32)
            sums += part
            squares += part * part
    mean = jnp.sum(sums, axis=-1, keepdims=True) / full
    var = jnp.sum(squares, axis=-1, keepdims=True) / full - mean * mean
    inv_std = lax.rsqrt(var + norm_epsilon)
    total = jnp.zeros((rows, width), F32)
    for pair in range(SIDE * SIDE // 2):
        value[2 * pair].wait()
        value[2 * pair + 1].wait()
        normed = []
        for one in (2 * pair, 2 * pair + 1):
            affine = held[one, rows : rows + 16, :].astype(F32)
            part = held[one, :rows, :].astype(F32)
            normed.append(((part - mean) * inv_std * affine[0:1] + affine[1:2]).astype(BF16))
        wide = jnp.concatenate(normed, axis=1)
        total += lax.dot_general(
            wide, wv[2 * pair * width : 2 * (pair + 1) * width, :], NN, preferred_element_type=F32
        )
    mixed = mix(weights, total.astype(BF16))

    def product(pair):
        out[2 * pair].wait()
        out[2 * pair + 1].wait()
        return lax.dot_general(
            mixed, wo[:, 2 * pair * width : 2 * (pair + 1) * width], NN, preferred_element_type=F32
        )

    give_parts(product, (p2a, p2b, p1, p3, p0), parts, sem_out, width)


def project(kernel, place, pieces, weights, w_value, w_out, rows):
    width = w_value.shape[1]
    half = jax.ShapeDtypeStruct((2, rows, width), BF16)
    whole = jax.ShapeDtypeStruct((4, rows, width), BF16)
    hbm = pl.BlockSpec(memory_space=pl.ANY)
    blocks = SIDE * SIDE
    flops = 4 * rows * width * width * blocks + 4 * rows * rows * width
    moved = 2 * 2 * width * width * blocks + 4 * rows * width * blocks
    return pl.pallas_call(
        kernel,
        out_shape=[half] * 2 + [whole] * 3,
        in_specs=[pl.BlockSpec(memory_space=pltpu.SMEM)]
        + [hbm] * 5
        + [pl.BlockSpec(memory_space=pltpu.VMEM)]
        + [hbm] * 2,
        out_specs=[hbm] * 5,
        scratch_shapes=[
            pltpu.VMEM((blocks, pieces[0].shape[1], width), BF16),
            pltpu.VMEM((blocks, rows, width), BF16),
            pltpu.VMEM((blocks * width, width), BF16),
            pltpu.VMEM((width, blocks * width), BF16),
            pltpu.SemaphoreType.DMA((blocks // 2,)),
            pltpu.SemaphoreType.DMA((blocks // 2,)),
            pltpu.SemaphoreType.DMA((blocks,)),
            pltpu.SemaphoreType.DMA((blocks,)),
        ],
        cost_estimate=pl.CostEstimate(flops=flops, bytes_accessed=moved, transcendentals=0),
        compiler_params=pltpu.CompilerParams(vmem_limit_bytes=VMEM_LIMIT),
    )(place, *pieces, weights, w_value, w_out)


def around(value):
    return turned(value, "z", -1), turned(value, "z", 2), turned(value, "z", 1)


def both_sides(value):
    return turned(value, "y", -1), turned(value, "y", 1)


def relayed(right, left):
    return turned(left[:2], "y", 1), turned(right[2:], "y", -1)


def joined(parts, by_left, by_right):
    _, _, p1, p3, p0 = parts
    p1 = jnp.concatenate([add(p1[:2], by_left), p1[2:]], axis=0)
    p3 = jnp.concatenate([p3[:2], add(p3[2:], by_right)], axis=0)
    return p1, p3, p0


def three(a, b, c):
    return (a.astype(F32) + b.astype(F32) + c.astype(F32)).astype(BF16)


def summed(value, axis):
    return value + turned(value, axis, 2) + turned(value, axis, 1) + turned(value, axis, -1)


def per_device(
    x_fwd,
    cotangent,
    ln_gain,
    ln_bias,
    w_value,
    w_out,
    scores_fwd,
    scores_bwd,
    stash_codes,
    stash_scales,
    evict,
):
    tokens, upstream = x_fwd[0], cotangent[0]
    rows, width = tokens.shape
    full = width * SIDE * SIDE
    value_proj, out_proj = w_value[0], w_out[0]
    place = jnp.stack([lax.axis_index("y"), lax.axis_index("z")]).astype(jnp.int32)

    ordered = lax.optimization_barrier
    affine = jnp.concatenate([ln_gain, ln_bias, jnp.zeros((14, width), BF16)], axis=0)
    tokens_affine = jnp.concatenate([tokens, affine], axis=0)
    near_up = lax.all_gather(upstream, "z", axis=0)
    right_up, left_up = both_sides(near_up)
    across = turned(tokens_affine, "y", 2)
    near_tok = lax.all_gather(tokens_affine, "z", axis=0)
    right_up, left_up, near_tok, across = ordered((right_up, left_up, near_tok, across))
    far_up = relayed(right_up, left_up)
    across_z = around(across)
    heads = scores_fwd.shape[1:]
    weights_fwd, weights_bwd = pl.pallas_call(
        weights_kernel,
        out_shape=[jax.ShapeDtypeStruct(heads, BF16)] * 2,
        compiler_params=pltpu.CompilerParams(vmem_limit_bytes=VMEM_LIMIT),
    )(scores_fwd[0], scores_bwd[0])

    far_up, near_tok, weights_bwd = ordered((far_up, near_tok, weights_bwd))
    right_tok, left_tok = both_sides(near_tok)

    projections = (value_proj, out_proj, rows)
    pieces_up = (near_up, right_up, left_up, *far_up)
    parts_bwd = project(bwd_kernel, place, pieces_up, weights_bwd, *projections)
    codes, scales = stash_codes[0], stash_scales[0]
    parts_bwd, across_z, codes, scales = ordered((parts_bwd, across_z, codes, scales))
    across_z = jnp.stack(across_z)
    blocks = scales.shape[0]
    scale_rows = blocks * rows // width
    fill = jnp.zeros((16 - scale_rows, width), BF16)
    stash = jnp.concatenate([codes, scales.reshape(scale_rows, width), fill])
    far_stash = mirrored(stash)
    passing_bwd = turned(parts_bwd[0], "y", 1), turned(parts_bwd[1], "y", -1)
    right_tok, left_tok, passing_bwd = ordered((right_tok, left_tok, passing_bwd))
    pieces_tok = (near_tok, right_tok, left_tok, across, across_z)
    p1, p3, p0 = joined(parts_bwd, *passing_bwd)
    by_left, by_right = turned(p1, "y", 1), turned(p3, "y", -1)
    parts_fwd = project(fwd_kernel, place, pieces_tok, weights_fwd, *projections)
    by_left, by_right, parts_fwd, far_stash = ordered((by_left, by_right, parts_fwd, far_stash))

    passing_fwd = turned(parts_fwd[0], "y", 1), turned(parts_fwd[1], "y", -1)
    by_left, by_right, passing_fwd = ordered((by_left, by_right, passing_fwd))
    q0, q1, q2, q3 = three(p0, by_left, by_right)
    r2, r1, r3 = turned(q2, "z", 2), turned(q1, "z", 1), turned(q3, "z", -1)
    p1, p3, p0 = joined(parts_fwd, *passing_fwd)
    by_left, by_right = turned(p1, "y", 1), turned(p3, "y", -1)
    by_left, by_right, r1, r2, r3 = ordered((by_left, by_right, r1, r2, r3))
    f0, f1, f2, f3 = three(p0, by_left, by_right)
    f0 = add(f0, tokens)
    s2, s1 = shifted_turned(f2, 2), shifted_turned(f1, 1)
    s3, s0 = shifted_turned(f3, -1), shifted_turned(f0, 0)

    keep_own = evict[0] == lax.axis_index("pipe")
    far_scales = far_stash[rows : rows + scale_rows].reshape(blocks, rows)
    held_codes = jnp.where(keep_own[:, None], codes, far_stash[:rows])
    held_scales = jnp.where(keep_own[None, :], scales, far_scales)
    stashed = (
        held_codes.astype(F32).reshape(rows, blocks, width // blocks)
        * held_scales.astype(F32).T[:, :, None]
    ).reshape(rows, width)

    grad_normed = q0.astype(F32) + r1.astype(F32) + r2.astype(F32) + r3.astype(F32)
    grad_scaled = grad_normed * ln_gain[0].astype(F32)
    sums = jnp.stack(
        [
            jnp.sum(stashed, axis=-1),
            jnp.sum(stashed * stashed, axis=-1),
            jnp.sum(grad_scaled, axis=-1),
            jnp.sum(grad_scaled * stashed, axis=-1),
        ]
    )
    sums, s2 = ordered((summed(sums, "z"), s2))
    sums = summed(sums, "y") / full
    stash_mean, square_mean, grad_mean, cross_mean = (sums[i][:, None] for i in range(4))
    inv_std = lax.rsqrt(square_mean - stash_mean * stash_mean + norm_epsilon)
    centred = (stashed - stash_mean) * inv_std
    grad_input = inv_std * (
        grad_scaled - grad_mean - centred * inv_std * (cross_mean - stash_mean * grad_mean)
    )
    grad_input = (upstream.astype(F32) + grad_input).astype(BF16)
    bwd_next = shifted(grad_input, "pipe", -1)

    fwd_next = s0.astype(F32) + s1.astype(F32) + s2.astype(F32) + s3.astype(F32)
    fwd_next = fwd_next.astype(BF16)
    return (fwd_next[None], bwd_next[None])


def solution(mesh):
    pipe = mesh.devices.shape[0]
    split = Mesh(mesh.devices.reshape(pipe, SIDE, SIDE), ("pipe", "y", "z"))
    tp = ("y", "z")
    placed = (
        P("pipe", None, tp),
        P("pipe", None, tp),
        P("pipe", tp),
        P("pipe", tp),
        P("pipe", None, tp),
        P("pipe", tp, None),
        P("pipe", tp, None, None),
        P("pipe", tp, None, None),
        P("pipe", None, tp),
        P("pipe", tp, None),
        P("pipe", None),
    )
    return jax.shard_map(
        per_device,
        mesh=split,
        in_specs=placed,
        out_specs=(P("pipe", None, tp), P("pipe", None, tp)),
        check_vma=False,
    )
```

profile of v0, /device:TPU:75, one launch (start us, length us, event | category | flops | bytes accessed | tf_op | source)
XLA Modules:
  0.0 214.1 jit_solution(17637923310801140025)
XLA Ops:
  0.6 18.7 %all_gather.9.near = bf16[4,256,384]{2,1,0:T(8,128)(2,1)S(1)} all-gather(bf16[1,256,384]{2,1,0:T(8,128)(2,1)} %param.12), channel_id=1, replica_groups=mesh['pipe'=16,'y'=4,'z'=4] {'z'}, dimensions={0}, use_global_device_ids=true | all-gather | bytes 983040 | tf_op jit(solution)/shard_map/all_gather | solution.py:293
  19.3 0.2 collective-permute-start
  19.5 1.3 collective-permute-start.1
  20.9 1.1 maximum_maximum_fusion
  21.9 3.3 %collective-permute-start.2 = (bf16[272,384]{1,0:T(8,128)(2,1)S(1)}, bf16[272,384]{1,0:T(8,128)(2,1)S(1)}, u32[]{:S(2)}, u32[]{:S(2)}) collective-permute-start(bf16[272,384]{1,0:T(8,128)(2,1)S(1)} %maximum_maximum_fusion), channel_id=1, source_target_pairs={{0,8},{4,12},{8,0},{12,4},{1,9},{5,13},{9,1},{13,5},{2,10},{6,14},... | collective-permute-start | bytes 626696 | tf_op jit(solution)/shard_map/ppermute | solution.py:18
  25.2 15.4 %all-gather = bf16[1088,384]{1,0:T(8,128)(2,1)S(1)} all-gather(bf16[272,384]{1,0:T(8,128)(2,1)S(1)} %maximum_maximum_fusion), channel_id=2, replica_groups=mesh['pipe'=16,'y'=4,'z'=4] {'z'}, dimensions={0}, use_global_device_ids=true | all-gather | bytes 1044480 | tf_op jit(solution)/shard_map/all_gather | solution.py:296
  40.9 1.5 collective-permute-start.4
  42.4 3.2 %shard_map.122 = (bf16[3,256,256]{2,1,0:T(8,128)(2,1)}, bf16[3,256,256]{2,1,0:T(8,128)(2,1)}) custom-call(f32[3,256,256]{2,1,0:T(8,128)} %bitcast.64, f32[3,256,256]{2,1,0:T(8,128)} %bitcast.65), custom_call_target="tpu_custom_call" | custom-call | tf_op jit(solution)/shard_map/pallas_call | solution.py:301
  45.6 3.4 %collective-permute-done.3.fa = bf16[2,256,384]{2,1,0:T(8,128)(2,1)S(1)} collective-permute-done((bf16[2,256,384]{2,1,0:T(8,128)(2,1)S(1)}, bf16[2,256,384]{2,1,0:T(8,128)(2,1)S(1)}, u32[]{:S(2)}, u32[]{:S(2)}) %collective-permute-start.3) | collective-permute-done | bytes 393248 | tf_op jit(solution)/shard_map/ppermute | solution.py:18
  48.9 2.5 %collective-permute-start.8 = (bf16[4,272,384]{2,1,0:T(8,128)(2,1)S(1)}, bf16[4,272,384]{2,1,0:T(8,128)(2,1)S(1)}, u32[]{:S(2)}, u32[]{:S(2)}) collective-permute-start(bf16[4,272,384]{2,1,0:T(8,128)(2,1)S(1)} %bitcast.58), channel_id=1, source_target_pairs={{0,12},{4,0},{8,4},{12,8},{1,13},{5,1},{9,5},{13,9},{2,14},{6,2},{... | collective-permute-start | bytes 2506760 | tf_op jit(solution)/shard_map/ppermute | solution.py:18
  51.5 0.6 pad_add_fusion.place
  52.1 1.5 collective-permute-start.5
  53.6 3.2 %collective-permute-start.6 = (bf16[272,384]{1,0:T(8,128)(2,1)S(1)}, bf16[272,384]{1,0:T(8,128)(2,1)S(1)}, u32[]{:S(2)}, u32[]{:S(2)}) collective-permute-start(bf16[272,384]{1,0:T(8,128)(2,1)S(1)} %collective-permute-done.2.fa), channel_id=1, source_target_pairs={{0,2},{1,3},{2,0},{3,1},{4,6},{5,7},{6,4},{7,5},{8,10},{9,11},{10,... | collective-permute-start | bytes 626696 | tf_op jit(solution)/shard_map/ppermute | solution.py:18
  56.8 1.5 collective-permute-start.7
  58.3 11.7 %shard_map.123 = (bf16[2,256,384]{2,1,0:T(8,128)(2,1)}, bf16[2,256,384]{2,1,0:T(8,128)(2,1)}, bf16[4,256,384]{2,1,0:T(8,128)(2,1)}, bf16[4,256,384]{2,1,0:T(8,128)(2,1)}, bf16[4,256,384]{2,1,0:T(8,128)(2,1)}) custom-call(s32[2]{0:T(128)} %pad_add_fusion.place, bf16[4,256,384]{2,1,0:T(8,128)(2,1)} %copy-done.1, bf16[4,256,384]{2,1,0:T(8,128)(2,1)} %copy-done.2, ...), custom_call_target="tpu_custom_call" | custom-call | flops 2516582400 | bytes 15728640 | tf_op jit(solution)/shard_map/pallas_call | solution.py:221
  70.1 0.1 collective-permute-start.10
  70.2 1.5 collective-permute-start.11
  71.7 1.0 slice.51
  72.7 1.0 slice.52
  73.8 6.9 %collective-permute-done.10 = bf16[2,256,384]{2,1,0:T(8,128)(2,1)S(1)} collective-permute-done((bf16[2,256,384]{2,1,0:T(8,128)(2,1)}, bf16[2,256,384]{2,1,0:T(8,128)(2,1)S(1)}, u32[]{:S(2)}, u32[]{:S(2)}) %collective-permute-start.10) | collective-permute-done | bytes 393248 | tf_op jit(solution)/shard_map/ppermute | solution.py:18
  80.7 0.1 add_convert_fusion.5
  81.1 0.4 copy-done.4
  81.6 0.3 copy-done.5
  82.0 3.0 %collective-permute-start.13 = (bf16[4,256,384]{2,1,0:T(8,128)(2,1)S(1)}, bf16[4,256,384]{2,1,0:T(8,128)(2,1)S(1)}, u32[]{:S(2)}, u32[]{:S(2)}) collective-permute-start(bf16[4,256,384]{2,1,0:T(8,128)(2,1)S(1)} %pad_maximum_fusion.1), channel_id=1, source_target_pairs={{0,12},{4,0},{8,4},{12,8},{1,13},{5,1},{9,5},{13,9},{2,14},{6,2},{... | collective-permute-start | bytes 2359304 | tf_op jit(solution)/shard_map/ppermute | solution.py:18
  85.0 0.1 maximum_maximum_fusion.1
  85.1 17.7 %collective-permute-start.14 = (bf16[272,384]{1,0:T(8,128)(2,1)S(1)}, bf16[272,384]{1,0:T(8,128)(2,1)S(1)}, u32[]{:S(2)}, u32[]{:S(2)}) collective-permute-start(bf16[272,384]{1,0:T(8,128)(2,1)S(1)} %maximum_maximum_fusion.1), channel_id=1, source_target_pairs={{0,240},{16,224},{32,208},{48,192},{64,176},{80,160},{96,144},{112... | collective-permute-start | bytes 626696 | tf_op jit(solution)/shard_map/ppermute | solution.py:39
  102.8 2.0 pad_maximum_fusion.4.fb
  104.8 13.7 %shard_map.124 = (bf16[2,256,384]{2,1,0:T(8,128)(2,1)}, bf16[2,256,384]{2,1,0:T(8,128)(2,1)}, bf16[4,256,384]{2,1,0:T(8,128)(2,1)}, bf16[4,256,384]{2,1,0:T(8,128)(2,1)}, bf16[4,256,384]{2,1,0:T(8,128)(2,1)}) custom-call(s32[2]{0:T(128)} %pad_add_fusion.place, bf16[4,272,384]{2,1,0:T(8,128)(2,1)} %bitcast.60, bf16[4,272,384]{2,1,0:T(8,128)(2,1)} %copy-done.4, ...), custom_call_target="tpu_custom_call" | custom-call | flops 2516582400 | bytes 15728640 | tf_op jit(solution)/shard_map/pallas_call | solution.py:221
  118.6 0.6 copy-done.22
  119.3 1.7 collective-permute-start.15
  121.0 0.6 collective-permute-start.16
  121.6 1.0 slice.55
  122.7 1.0 slice.56
  123.7 7.6 %collective-permute-done.15 = bf16[2,256,384]{2,1,0:T(8,128)(2,1)S(1)} collective-permute-done((bf16[2,256,384]{2,1,0:T(8,128)(2,1)}, bf16[2,256,384]{2,1,0:T(8,128)(2,1)S(1)}, u32[]{:S(2)}, u32[]{:S(2)}) %collective-permute-start.15) | collective-permute-done | bytes 393248 | tf_op jit(solution)/shard_map/ppermute | solution.py:18
  131.3 1.0 collective-permute-done.16
  132.6 1.1 collective-permute-start.17
  133.8 0.8 collective-permute-start.18
  134.7 1.7 add_convert_fusion.1
  136.4 0.8 slice_bitcast_fusion.5
  137.2 2.5 %collective-permute-start.20 = (bf16[256,384]{1,0:T(8,128)(2,1)}, bf16[256,384]{1,0:T(8,128)(2,1)}, u32[]{:S(2)}, u32[]{:S(2)}) collective-permute-start(bf16[256,384]{1,0:T(8,128)(2,1)} %get-tuple-element.118), channel_id=1, source_target_pairs={{0,2},{1,3},{2,0},{3,1},{4,6},{5,7},{6,4},{7,5},{8,10},{9,11},{10,... | collective-permute-start | bytes 589832 | tf_op jit(solution)/shard_map/ppermute | solution.py:18
  139.7 2.4 %collective-permute-start.21 = (bf16[256,384]{1,0:T(8,128)(2,1)}, bf16[256,384]{1,0:T(8,128)(2,1)}, u32[]{:S(2)}, u32[]{:S(2)}) collective-permute-start(bf16[256,384]{1,0:T(8,128)(2,1)} %get-tuple-element.117), channel_id=1, source_target_pairs={{0,3},{1,0},{2,1},{3,2},{4,7},{5,4},{6,5},{7,6},{8,11},{9,8},{10,9... | collective-permute-start | bytes 589832 | tf_op jit(solution)/shard_map/ppermute | solution.py:18
  142.1 0.2 copy.15
  142.3 6.3 %collective-permute-done.19 = bf16[256,384]{1,0:T(8,128)(2,1)} collective-permute-done((bf16[256,384]{1,0:T(8,128)(2,1)}, bf16[256,384]{1,0:T(8,128)(2,1)}, u32[]{:S(2)}, u32[]{:S(2)}) %collective-permute-start.19) | collective-permute-done | bytes 196640 | tf_op jit(solution)/shard_map/ppermute | solution.py:18
  148.6 6.0 %collective-permute-done.20 = bf16[256,384]{1,0:T(8,128)(2,1)} collective-permute-done((bf16[256,384]{1,0:T(8,128)(2,1)}, bf16[256,384]{1,0:T(8,128)(2,1)}, u32[]{:S(2)}, u32[]{:S(2)}) %collective-permute-start.20) | collective-permute-done | bytes 196640 | tf_op jit(solution)/shard_map/ppermute | solution.py:18
  154.6 5.8 %collective-permute-done.21 = bf16[256,384]{1,0:T(8,128)(2,1)} collective-permute-done((bf16[256,384]{1,0:T(8,128)(2,1)}, bf16[256,384]{1,0:T(8,128)(2,1)}, u32[]{:S(2)}, u32[]{:S(2)}) %collective-permute-start.21) | collective-permute-done | bytes 196640 | tf_op jit(solution)/shard_map/ppermute | solution.py:18
  160.4 1.6 fusion.6
  162.1 1.4 collective-permute-start.26
  163.5 2.3 %collective-permute-start.25 = (f32[4,256]{1,0:T(4,128)S(1)}, f32[4,256]{1,0:T(4,128)S(1)}, u32[]{:S(2)}, u32[]{:S(2)}) collective-permute-start(f32[4,256]{1,0:T(4,128)S(1)} %pad_maximum_fusion.5), channel_id=1, source_target_pairs={{0,1},{1,2},{2,3},{3,0},{4,5},{5,6},{6,7},{7,4},{8,9},{9,10},{10,1... | collective-permute-start | bytes 12296 | tf_op jit(solution)/shard_map/ppermute | solution.py:18
  165.7 3.0 %collective-permute-start.24 = (f32[4,256]{1,0:T(4,128)S(1)}, f32[4,256]{1,0:T(4,128)S(1)}, u32[]{:S(2)}, u32[]{:S(2)}) collective-permute-start(f32[4,256]{1,0:T(4,128)S(1)} %pad_maximum_fusion.5), channel_id=1, source_target_pairs={{0,2},{1,3},{2,0},{3,1},{4,6},{5,7},{6,4},{7,5},{8,10},{9,11},{10,... | collective-permute-start | bytes 12296 | tf_op jit(solution)/shard_map/ppermute | solution.py:18
  168.7 1.7 add_convert_fusion
  170.4 6.7 %collective-permute-start.27 = (bf16[256,384]{1,0:T(8,128)(2,1)S(1)}, bf16[256,384]{1,0:T(8,128)(2,1)S(1)}, u32[]{:S(2)}, u32[]{:S(2)}) collective-permute-start(bf16[256,384]{1,0:T(8,128)(2,1)S(1)} %get-tuple-element.116), channel_id=1, source_target_pairs={{0,18},{1,19},{2,16},{3,17},{16,34},{17,35},{18,32},{19,33},{32,50... | collective-permute-start | bytes 589832 | tf_op jit(solution)/shard_map/ppermute | solution.py:34
  177.2 9.4 %collective-permute-done.27 = bf16[256,384]{1,0:T(8,128)(2,1)S(1)} collective-permute-done((bf16[256,384]{1,0:T(8,128)(2,1)S(1)}, bf16[256,384]{1,0:T(8,128)(2,1)S(1)}, u32[]{:S(2)}, u32[]{:S(2)}) %collective-permute-start.27) | collective-permute-done | bytes 196640 | tf_op jit(solution)/shard_map/ppermute | solution.py:34
  186.5 2.9 %collective-permute-start.31 = (f32[4,256]{1,0:T(4,128)S(1)}, f32[4,256]{1,0:T(4,128)S(1)}, u32[]{:S(2)}, u32[]{:S(2)}) collective-permute-start(f32[4,256]{1,0:T(4,128)S(1)} %add_add_fusion), channel_id=1, source_target_pairs={{0,12},{4,0},{8,4},{12,8},{1,13},{5,1},{9,5},{13,9},{2,14},{6,2},{... | collective-permute-start | bytes 12296 | tf_op jit(solution)/shard_map/ppermute | solution.py:18
  189.5 3.2 %collective-permute-start.29 = (f32[4,256]{1,0:T(4,128)S(1)}, f32[4,256]{1,0:T(4,128)S(1)}, u32[]{:S(2)}, u32[]{:S(2)}) collective-permute-start(f32[4,256]{1,0:T(4,128)S(1)} %add_add_fusion), channel_id=1, source_target_pairs={{0,8},{4,12},{8,0},{12,4},{1,9},{5,13},{9,1},{13,5},{2,10},{6,14},... | collective-permute-start | bytes 12296 | tf_op jit(solution)/shard_map/ppermute | solution.py:18
  192.8 1.9 collective-permute-start.28
  194.7 7.0 %collective-permute-start.23 = (bf16[256,384]{1,0:T(8,128)(2,1)S(1)}, bf16[256,384]{1,0:T(8,128)(2,1)S(1)}, u32[]{:S(2)}, u32[]{:S(2)}) collective-permute-start(bf16[256,384]{1,0:T(8,128)(2,1)S(1)} %get-tuple-element.114), channel_id=1, source_target_pairs={{0,17},{1,18},{2,19},{3,16},{16,33},{17,34},{18,35},{19,32},{32,49... | collective-permute-start | bytes 589832 | tf_op jit(solution)/shard_map/ppermute | solution.py:34
  201.7 4.4 %collective-permute-start.22 = (bf16[256,384]{1,0:T(8,128)(2,1)S(1)}, bf16[256,384]{1,0:T(8,128)(2,1)S(1)}, u32[]{:S(2)}, u32[]{:S(2)}) collective-permute-start(bf16[256,384]{1,0:T(8,128)(2,1)S(1)} %fusion.4), channel_id=1, source_target_pairs={{0,16},{1,17},{2,18},{3,19},{16,32},{17,33},{18,34},{19,35},{32,48... | collective-permute-start | bytes 589832 | tf_op jit(solution)/shard_map/ppermute | solution.py:34
  206.2 0.2 fusion
  206.5 1.9 collective-permute-start.32
  208.4 0.7 collective-permute-done.23
  209.1 0.5 collective-permute-done.22
  209.6 0.8 fusion.5
  210.4 3.1 %collective-permute-done.32 = bf16[256,384]{1,0:T(8,128)(2,1)S(1)} collective-permute-done((bf16[256,384]{1,0:T(8,128)(2,1)S(1)}, bf16[256,384]{1,0:T(8,128)(2,1)S(1)}, u32[]{:S(2)}, u32[]{:S(2)}) %collective-permute-start.32) | collective-permute-done | bytes 196640 | tf_op jit(solution)/shard_map/ppermute | solution.py:24
  213.4 0.7 copy.17
  (102 shorter events, 1.5 us)
Async XLA Ops:
  19.3 26.3 %copy-start.1 = (bf16[4,256,384]{2,1,0:T(8,128)(2,1)}, bf16[4,256,384]{2,1,0:T(8,128)(2,1)S(1)}, u32[]{:S(2)}) copy-start(bf16[4,256,384]{2,1,0:T(8,128)(2,1)S(1)} %all_gather.9.near) | copy-start | bytes 2359300
  19.3 21.3 %collective-permute-start = (bf16[4,256,384]{2,1,0:T(8,128)(2,1)S(1)}, bf16[4,256,384]{2,1,0:T(8,128)(2,1)S(1)}, u32[]{:S(2)}, u32[]{:S(2)}) collective-permute-start(bf16[4,256,384]{2,1,0:T(8,128)(2,1)S(1)} %all_gather.9.near), channel_id=1, source_target_pairs={{0,12},{4,0},{8,4},{12,8},{1,13},{5,1},{9,5},{13,9},{2,14},{6,2},{... | collective-permute-start | bytes 2359304 | tf_op jit(solution)/shard_map/ppermute | solution.py:18
  19.5 21.2 %collective-permute-start.1 = (bf16[4,256,384]{2,1,0:T(8,128)(2,1)S(1)}, bf16[4,256,384]{2,1,0:T(8,128)(2,1)S(1)}, u32[]{:S(2)}, u32[]{:S(2)}) collective-permute-start(bf16[4,256,384]{2,1,0:T(8,128)(2,1)S(1)} %all_gather.9.near), channel_id=1, source_target_pairs={{0,4},{4,8},{8,12},{12,0},{1,5},{5,9},{9,13},{13,1},{2,6},{6,10},{... | collective-permute-start | bytes 2359304 | tf_op jit(solution)/shard_map/ppermute | solution.py:18
  21.9 18.7 %collective-permute-start.2 = (bf16[272,384]{1,0:T(8,128)(2,1)S(1)}, bf16[272,384]{1,0:T(8,128)(2,1)S(1)}, u32[]{:S(2)}, u32[]{:S(2)}) collective-permute-start(bf16[272,384]{1,0:T(8,128)(2,1)S(1)} %maximum_maximum_fusion), channel_id=1, source_target_pairs={{0,8},{4,12},{8,0},{12,4},{1,9},{5,13},{9,1},{13,5},{2,10},{6,14},... | collective-permute-start | bytes 626696 | tf_op jit(solution)/shard_map/ppermute | solution.py:18
  40.6 10.8 %copy-start = (bf16[1088,384]{1,0:T(8,128)(2,1)}, bf16[1088,384]{1,0:T(8,128)(2,1)S(1)}, u32[]{:S(2)}) copy-start(bf16[1088,384]{1,0:T(8,128)(2,1)S(1)} %all-gather) | copy-start | bytes 2506756
  40.6 16.2 %copy-start.21 = (bf16[272,384]{1,0:T(8,128)(2,1)}, bf16[272,384]{1,0:T(8,128)(2,1)S(1)}, u32[]{:S(2)}) copy-start(bf16[272,384]{1,0:T(8,128)(2,1)S(1)} %collective-permute-done.2.fa) | copy-start | bytes 626692
  40.6 4.9 %copy-start.2 = (bf16[4,256,384]{2,1,0:T(8,128)(2,1)}, bf16[4,256,384]{2,1,0:T(8,128)(2,1)S(1)}, u32[]{:S(2)}) copy-start(bf16[4,256,384]{2,1,0:T(8,128)(2,1)S(1)} %collective-permute-done.right) | copy-start | bytes 2359300
  40.7 4.9 %copy-start.3 = (bf16[4,256,384]{2,1,0:T(8,128)(2,1)}, bf16[4,256,384]{2,1,0:T(8,128)(2,1)S(1)}, u32[]{:S(2)}) copy-start(bf16[4,256,384]{2,1,0:T(8,128)(2,1)S(1)} %collective-permute-done.1.left) | copy-start | bytes 2359300
  40.7 8.2 %collective-permute-start.3 = (bf16[2,256,384]{2,1,0:T(8,128)(2,1)S(1)}, bf16[2,256,384]{2,1,0:T(8,128)(2,1)S(1)}, u32[]{:S(2)}, u32[]{:S(2)}) collective-permute-start(bf16[2,256,384]{2,1,0:T(8,128)(2,1)S(1)} %slice.48), channel_id=1, source_target_pairs={{0,4},{4,8},{8,12},{12,0},{1,5},{5,9},{9,13},{13,1},{2,6},{6,10},{... | collective-permute-start | bytes 1179656 | tf_op jit(solution)/shard_map/ppermute | solution.py:18
  40.9 8.1 %collective-permute-start.4 = (bf16[2,256,384]{2,1,0:T(8,128)(2,1)S(1)}, bf16[2,256,384]{2,1,0:T(8,128)(2,1)S(1)}, u32[]{:S(2)}, u32[]{:S(2)}) collective-permute-start(bf16[2,256,384]{2,1,0:T(8,128)(2,1)S(1)} %slice.49), channel_id=1, source_target_pairs={{0,12},{4,0},{8,4},{12,8},{1,13},{5,1},{9,5},{13,9},{2,14},{6,2},{... | collective-permute-start | bytes 1179656 | tf_op jit(solution)/shard_map/ppermute | solution.py:18
  48.9 2.5 %copy-start.16 = (bf16[2,256,384]{2,1,0:T(8,128)(2,1)}, bf16[2,256,384]{2,1,0:T(8,128)(2,1)S(1)}, u32[]{:S(2)}) copy-start(bf16[2,256,384]{2,1,0:T(8,128)(2,1)S(1)} %collective-permute-done.3.fa) | copy-start | bytes 1179652
  48.9 2.5 %copy-start.17 = (bf16[2,256,384]{2,1,0:T(8,128)(2,1)}, bf16[2,256,384]{2,1,0:T(8,128)(2,1)S(1)}, u32[]{:S(2)}) copy-start(bf16[2,256,384]{2,1,0:T(8,128)(2,1)S(1)} %collective-permute-done.4.fb) | copy-start | bytes 1179652
  48.9 31.7 %collective-permute-start.8 = (bf16[4,272,384]{2,1,0:T(8,128)(2,1)S(1)}, bf16[4,272,384]{2,1,0:T(8,128)(2,1)S(1)}, u32[]{:S(2)}, u32[]{:S(2)}) collective-permute-start(bf16[4,272,384]{2,1,0:T(8,128)(2,1)S(1)} %bitcast.58), channel_id=1, source_target_pairs={{0,12},{4,0},{8,4},{12,8},{1,13},{5,1},{9,5},{13,9},{2,14},{6,2},{... | collective-permute-start | bytes 2506760 | tf_op jit(solution)/shard_map/ppermute | solution.py:18
  51.5 29.2 %collective-permute-start.9 = (bf16[4,272,384]{2,1,0:T(8,128)(2,1)S(1)}, bf16[4,272,384]{2,1,0:T(8,128)(2,1)S(1)}, u32[]{:S(2)}, u32[]{:S(2)}) collective-permute-start(bf16[4,272,384]{2,1,0:T(8,128)(2,1)S(1)} %bitcast.59), channel_id=1, source_target_pairs={{0,4},{4,8},{8,12},{12,0},{1,5},{5,9},{9,13},{13,1},{2,6},{6,10},{... | collective-permute-start | bytes 2506760 | tf_op jit(solution)/shard_map/ppermute | solution.py:18
  52.1 17.9 %collective-permute-start.5 = (bf16[272,384]{1,0:T(8,128)(2,1)S(1)}, bf16[272,384]{1,0:T(8,128)(2,1)S(1)}, u32[]{:S(2)}, u32[]{:S(2)}) collective-permute-start(bf16[272,384]{1,0:T(8,128)(2,1)S(1)} %collective-permute-done.2.fa), channel_id=1, source_target_pairs={{0,3},{1,0},{2,1},{3,2},{4,7},{5,4},{6,5},{7,6},{8,11},{9,8},{10,9... | collective-permute-start | bytes 626696 | tf_op jit(solution)/shard_map/ppermute | solution.py:18
  53.6 16.5 %collective-permute-start.6 = (bf16[272,384]{1,0:T(8,128)(2,1)S(1)}, bf16[272,384]{1,0:T(8,128)(2,1)S(1)}, u32[]{:S(2)}, u32[]{:S(2)}) collective-permute-start(bf16[272,384]{1,0:T(8,128)(2,1)S(1)} %collective-permute-done.2.fa), channel_id=1, source_target_pairs={{0,2},{1,3},{2,0},{3,1},{4,6},{5,7},{6,4},{7,5},{8,10},{9,11},{10,... | collective-permute-start | bytes 626696 | tf_op jit(solution)/shard_map/ppermute | solution.py:18
  56.8 13.3 %collective-permute-start.7 = (bf16[272,384]{1,0:T(8,128)(2,1)S(1)}, bf16[272,384]{1,0:T(8,128)(2,1)S(1)}, u32[]{:S(2)}, u32[]{:S(2)}) collective-permute-start(bf16[272,384]{1,0:T(8,128)(2,1)S(1)} %collective-permute-done.2.fa), channel_id=1, source_target_pairs={{0,1},{1,2},{2,3},{3,0},{4,5},{5,6},{6,7},{7,4},{8,9},{9,10},{10,1... | collective-permute-start | bytes 626696 | tf_op jit(solution)/shard_map/ppermute | solution.py:18
  70.0 10.7 %copy-start.10 = (bf16[4,256,384]{2,1,0:T(8,128)(2,1)S(1)}, bf16[4,256,384]{2,1,0:T(8,128)(2,1)}, u32[]{:S(2)}) copy-start(bf16[4,256,384]{2,1,0:T(8,128)(2,1)} %get-tuple-element.68) | copy-start | bytes 2359300
  70.0 11.9 %copy-start.18 = (bf16[272,384]{1,0:T(8,128)(2,1)}, bf16[272,384]{1,0:T(8,128)(2,1)S(1)}, u32[]{:S(2)}) copy-start(bf16[272,384]{1,0:T(8,128)(2,1)S(1)} %collective-permute-done.5) | copy-start | bytes 626692
  70.0 11.9 %copy-start.19 = (bf16[272,384]{1,0:T(8,128)(2,1)}, bf16[272,384]{1,0:T(8,128)(2,1)S(1)}, u32[]{:S(2)}) copy-start(bf16[272,384]{1,0:T(8,128)(2,1)S(1)} %collective-permute-done.6) | copy-start | bytes 626692
  70.1 11.9 %copy-start.20 = (bf16[272,384]{1,0:T(8,128)(2,1)}, bf16[272,384]{1,0:T(8,128)(2,1)S(1)}, u32[]{:S(2)}) copy-start(bf16[272,384]{1,0:T(8,128)(2,1)S(1)} %collective-permute-done.7) | copy-start | bytes 626692
  70.1 10.6 %collective-permute-start.10 = (bf16[2,256,384]{2,1,0:T(8,128)(2,1)}, bf16[2,256,384]{2,1,0:T(8,128)(2,1)S(1)}, u32[]{:S(2)}, u32[]{:S(2)}) collective-permute-start(bf16[2,256,384]{2,1,0:T(8,128)(2,1)} %get-tuple-element.70), channel_id=1, source_target_pairs={{0,4},{4,8},{8,12},{12,0},{1,5},{5,9},{9,13},{13,1},{2,6},{6,10},{... | collective-permute-start | bytes 1179656 | tf_op jit(solution)/shard_map/ppermute | solution.py:18
  70.2 10.5 %collective-permute-start.11 = (bf16[2,256,384]{2,1,0:T(8,128)(2,1)}, bf16[2,256,384]{2,1,0:T(8,128)(2,1)S(1)}, u32[]{:S(2)}, u32[]{:S(2)}) collective-permute-start(bf16[2,256,384]{2,1,0:T(8,128)(2,1)} %get-tuple-element.71), channel_id=1, source_target_pairs={{0,12},{4,0},{8,4},{12,8},{1,13},{5,1},{9,5},{13,9},{2,14},{6,2},{... | collective-permute-start | bytes 1179656 | tf_op jit(solution)/shard_map/ppermute | solution.py:18
  73.8 7.3 %copy-start.8 = (bf16[4,256,384]{2,1,0:T(8,128)(2,1)S(1)}, bf16[4,256,384]{2,1,0:T(8,128)(2,1)}, u32[]{:S(2)}) copy-start(bf16[4,256,384]{2,1,0:T(8,128)(2,1)} %get-tuple-element.73) | copy-start | bytes 2359300
  80.7 0.9 copy-start.4
  80.7 1.2 copy-start.5
  80.9 4.1 %copy-start.23 = (bf16[1,3,256]{2,1,0:T(4,128)(2,1)S(1)}, bf16[1,3,256]{2,1,0:T(4,128)(2,1)}, u32[]{:S(2)}) copy-start(bf16[1,3,256]{2,1,0:T(4,128)(2,1)} %param.20) | copy-start | bytes 4612
  80.9 4.1 %copy-start.6 = (bf16[1,256,384]{2,1,0:T(8,128)(2,1)S(1)}, bf16[1,256,384]{2,1,0:T(8,128)(2,1)}, u32[]{:S(2)}) copy-start(bf16[1,256,384]{2,1,0:T(8,128)(2,1)} %param.19) | copy-start | bytes 589828
  80.9 37.7 %collective-permute-start.12 = (bf16[4,256,384]{2,1,0:T(8,128)(2,1)S(1)}, bf16[4,256,384]{2,1,0:T(8,128)(2,1)}, u32[]{:S(2)}, u32[]{:S(2)}) collective-permute-start(bf16[4,256,384]{2,1,0:T(8,128)(2,1)S(1)} %pad_maximum_fusion), channel_id=1, source_target_pairs={{0,4},{4,8},{8,12},{12,0},{1,5},{5,9},{9,13},{13,1},{2,6},{6,10},{... | collective-permute-start | bytes 2359304 | tf_op jit(solution)/shard_map/ppermute | solution.py:18
  82.0 36.7 %collective-permute-start.13 = (bf16[4,256,384]{2,1,0:T(8,128)(2,1)S(1)}, bf16[4,256,384]{2,1,0:T(8,128)(2,1)S(1)}, u32[]{:S(2)}, u32[]{:S(2)}) collective-permute-start(bf16[4,256,384]{2,1,0:T(8,128)(2,1)S(1)} %pad_maximum_fusion.1), channel_id=1, source_target_pairs={{0,12},{4,0},{8,4},{12,8},{1,13},{5,1},{9,5},{13,9},{2,14},{6,2},{... | collective-permute-start | bytes 2359304 | tf_op jit(solution)/shard_map/ppermute | solution.py:18
  85.1 33.5 %collective-permute-start.14 = (bf16[272,384]{1,0:T(8,128)(2,1)S(1)}, bf16[272,384]{1,0:T(8,128)(2,1)S(1)}, u32[]{:S(2)}, u32[]{:S(2)}) collective-permute-start(bf16[272,384]{1,0:T(8,128)(2,1)S(1)} %maximum_maximum_fusion.1), channel_id=1, source_target_pairs={{0,240},{16,224},{32,208},{48,192},{64,176},{80,160},{96,144},{112... | collective-permute-start | bytes 626696 | tf_op jit(solution)/shard_map/ppermute | solution.py:39
  104.8 16.8 %copy-start.24 = (bf16[1,384]{1,0:T(2,128)(2,1)S(1)}, bf16[1,384]{1,0:T(2,128)(2,1)}, u32[]{:S(2)}) copy-start(bf16[1,384]{1,0:T(2,128)(2,1)} %param.13) | copy-start | bytes 2308
  118.6 13.7 %copy-start.9 = (bf16[4,256,384]{2,1,0:T(8,128)(2,1)S(1)}, bf16[4,256,384]{2,1,0:T(8,128)(2,1)}, u32[]{:S(2)}) copy-start(bf16[4,256,384]{2,1,0:T(8,128)(2,1)} %get-tuple-element.89) | copy-start | bytes 2359300
  118.6 0.7 copy-start.22
  118.6 13.7 %copy-start.14 = (bf16[4,256,384]{2,1,0:T(8,128)(2,1)}, bf16[4,256,384]{2,1,0:T(8,128)(2,1)S(1)}, u32[]{:S(2)}) copy-start(bf16[4,256,384]{2,1,0:T(8,128)(2,1)S(1)} %collective-permute-done.13) | copy-start | bytes 2359300
  119.3 12.0 %collective-permute-start.15 = (bf16[2,256,384]{2,1,0:T(8,128)(2,1)}, bf16[2,256,384]{2,1,0:T(8,128)(2,1)S(1)}, u32[]{:S(2)}, u32[]{:S(2)}) collective-permute-start(bf16[2,256,384]{2,1,0:T(8,128)(2,1)} %get-tuple-element.92), channel_id=1, source_target_pairs={{0,4},{4,8},{8,12},{12,0},{1,5},{5,9},{9,13},{13,1},{2,6},{6,10},{... | collective-permute-start | bytes 1179656 | tf_op jit(solution)/shard_map/ppermute | solution.py:18
  121.0 11.3 %collective-permute-start.16 = (bf16[2,256,384]{2,1,0:T(8,128)(2,1)}, bf16[2,256,384]{2,1,0:T(8,128)(2,1)S(1)}, u32[]{:S(2)}, u32[]{:S(2)}) collective-permute-start(bf16[2,256,384]{2,1,0:T(8,128)(2,1)} %get-tuple-element.93), channel_id=1, source_target_pairs={{0,12},{4,0},{8,4},{12,8},{1,13},{5,1},{9,5},{13,9},{2,14},{6,2},{... | collective-permute-start | bytes 1179656 | tf_op jit(solution)/shard_map/ppermute | solution.py:18
  123.7 9.9 %copy-start.7 = (bf16[4,256,384]{2,1,0:T(8,128)(2,1)S(1)}, bf16[4,256,384]{2,1,0:T(8,128)(2,1)}, u32[]{:S(2)}) copy-start(bf16[4,256,384]{2,1,0:T(8,128)(2,1)} %get-tuple-element.95) | copy-start | bytes 2359300
  132.5 2.1 copy-start.25
  132.5 2.1 slice-start
  132.6 2.1 %copy-start.12 = (bf16[4,256,384]{2,1,0:T(8,128)(2,1)S(1)}, bf16[4,256,384]{2,1,0:T(8,128)(2,1)}, u32[]{:S(2)}) copy-start(bf16[4,256,384]{2,1,0:T(8,128)(2,1)} %get-tuple-element.97) | copy-start | bytes 2359300
  132.6 27.8 %collective-permute-start.17 = (bf16[4,256,384]{2,1,0:T(8,128)(2,1)S(1)}, bf16[4,256,384]{2,1,0:T(8,128)(2,1)}, u32[]{:S(2)}, u32[]{:S(2)}) collective-permute-start(bf16[4,256,384]{2,1,0:T(8,128)(2,1)S(1)} %pad_maximum_fusion.2), channel_id=1, source_target_pairs={{0,4},{4,8},{8,12},{12,0},{1,5},{5,9},{9,13},{13,1},{2,6},{6,10},{... | collective-permute-start | bytes 2359304 | tf_op jit(solution)/shard_map/ppermute | solution.py:18
  133.8 26.6 %collective-permute-start.18 = (bf16[4,256,384]{2,1,0:T(8,128)(2,1)S(1)}, bf16[4,256,384]{2,1,0:T(8,128)(2,1)}, u32[]{:S(2)}, u32[]{:S(2)}) collective-permute-start(bf16[4,256,384]{2,1,0:T(8,128)(2,1)S(1)} %pad_maximum_fusion.3), channel_id=1, source_target_pairs={{0,12},{4,0},{8,4},{12,8},{1,13},{5,1},{9,5},{13,9},{2,14},{6,2},{... | collective-permute-start | bytes 2359304 | tf_op jit(solution)/shard_map/ppermute | solution.py:18
  137.2 11.4 %collective-permute-start.19 = (bf16[256,384]{1,0:T(8,128)(2,1)}, bf16[256,384]{1,0:T(8,128)(2,1)}, u32[]{:S(2)}, u32[]{:S(2)}) collective-permute-start(bf16[256,384]{1,0:T(8,128)(2,1)} %get-tuple-element.119), channel_id=1, source_target_pairs={{0,1},{1,2},{2,3},{3,0},{4,5},{5,6},{6,7},{7,4},{8,9},{9,10},{10,1... | collective-permute-start | bytes 589832 | tf_op jit(solution)/shard_map/ppermute | solution.py:18
  137.2 17.4 %collective-permute-start.20 = (bf16[256,384]{1,0:T(8,128)(2,1)}, bf16[256,384]{1,0:T(8,128)(2,1)}, u32[]{:S(2)}, u32[]{:S(2)}) collective-permute-start(bf16[256,384]{1,0:T(8,128)(2,1)} %get-tuple-element.118), channel_id=1, source_target_pairs={{0,2},{1,3},{2,0},{3,1},{4,6},{5,7},{6,4},{7,5},{8,10},{9,11},{10,... | collective-permute-start | bytes 589832 | tf_op jit(solution)/shard_map/ppermute | solution.py:18
  139.7 20.7 %collective-permute-start.21 = (bf16[256,384]{1,0:T(8,128)(2,1)}, bf16[256,384]{1,0:T(8,128)(2,1)}, u32[]{:S(2)}, u32[]{:S(2)}) collective-permute-start(bf16[256,384]{1,0:T(8,128)(2,1)} %get-tuple-element.117), channel_id=1, source_target_pairs={{0,3},{1,0},{2,1},{3,2},{4,7},{5,4},{6,5},{7,6},{8,11},{9,8},{10,9... | collective-permute-start | bytes 589832 | tf_op jit(solution)/shard_map/ppermute | solution.py:18
  142.3 26.4 %copy-start.13 = (bf16[4,256,384]{2,1,0:T(8,128)(2,1)S(1)}, bf16[4,256,384]{2,1,0:T(8,128)(2,1)}, u32[]{:S(2)}) copy-start(bf16[4,256,384]{2,1,0:T(8,128)(2,1)} %get-tuple-element.88) | copy-start | bytes 2359300
  162.0 30.7 %copy-start.11 = (bf16[1,256,384]{2,1,0:T(8,128)(2,1)S(1)}, bf16[1,256,384]{2,1,0:T(8,128)(2,1)}, u32[]{:S(2)}) copy-start(bf16[1,256,384]{2,1,0:T(8,128)(2,1)} %param.11) | copy-start | bytes 589828
  162.1 15.1 %collective-permute-start.26 = (f32[4,256]{1,0:T(4,128)S(1)}, f32[4,256]{1,0:T(4,128)S(1)}, u32[]{:S(2)}, u32[]{:S(2)}) collective-permute-start(f32[4,256]{1,0:T(4,128)S(1)} %pad_maximum_fusion.5), channel_id=1, source_target_pairs={{0,3},{1,0},{2,1},{3,2},{4,7},{5,4},{6,5},{7,6},{8,11},{9,8},{10,9... | collective-permute-start | bytes 12296 | tf_op jit(solution)/shard_map/ppermute | solution.py:18
  163.5 13.7 %collective-permute-start.25 = (f32[4,256]{1,0:T(4,128)S(1)}, f32[4,256]{1,0:T(4,128)S(1)}, u32[]{:S(2)}, u32[]{:S(2)}) collective-permute-start(f32[4,256]{1,0:T(4,128)S(1)} %pad_maximum_fusion.5), channel_id=1, source_target_pairs={{0,1},{1,2},{2,3},{3,0},{4,5},{5,6},{6,7},{7,4},{8,9},{9,10},{10,1... | collective-permute-start | bytes 12296 | tf_op jit(solution)/shard_map/ppermute | solution.py:18
  165.7 11.4 %collective-permute-start.24 = (f32[4,256]{1,0:T(4,128)S(1)}, f32[4,256]{1,0:T(4,128)S(1)}, u32[]{:S(2)}, u32[]{:S(2)}) collective-permute-start(f32[4,256]{1,0:T(4,128)S(1)} %pad_maximum_fusion.5), channel_id=1, source_target_pairs={{0,2},{1,3},{2,0},{3,1},{4,6},{5,7},{6,4},{7,5},{8,10},{9,11},{10,... | collective-permute-start | bytes 12296 | tf_op jit(solution)/shard_map/ppermute | solution.py:18
  170.4 35.9 %copy-start.15 = (bf16[1,256,384]{2,1,0:T(8,128)(2,1)S(1)}, bf16[1,256,384]{2,1,0:T(8,128)(2,1)}, u32[]{:S(2)}) copy-start(bf16[1,256,384]{2,1,0:T(8,128)(2,1)} %param.12) | copy-start | bytes 589828
  170.4 16.1 %collective-permute-start.27 = (bf16[256,384]{1,0:T(8,128)(2,1)S(1)}, bf16[256,384]{1,0:T(8,128)(2,1)S(1)}, u32[]{:S(2)}, u32[]{:S(2)}) collective-permute-start(bf16[256,384]{1,0:T(8,128)(2,1)S(1)} %get-tuple-element.116), channel_id=1, source_target_pairs={{0,18},{1,19},{2,16},{3,17},{16,34},{17,35},{18,32},{19,33},{32,50... | collective-permute-start | bytes 589832 | tf_op jit(solution)/shard_map/ppermute | solution.py:34
  186.5 15.2 %collective-permute-start.31 = (f32[4,256]{1,0:T(4,128)S(1)}, f32[4,256]{1,0:T(4,128)S(1)}, u32[]{:S(2)}, u32[]{:S(2)}) collective-permute-start(f32[4,256]{1,0:T(4,128)S(1)} %add_add_fusion), channel_id=1, source_target_pairs={{0,12},{4,0},{8,4},{12,8},{1,13},{5,1},{9,5},{13,9},{2,14},{6,2},{... | collective-permute-start | bytes 12296 | tf_op jit(solution)/shard_map/ppermute | solution.py:18
  189.5 16.7 %collective-permute-start.30 = (f32[4,256]{1,0:T(4,128)S(1)}, f32[4,256]{1,0:T(4,128)S(1)}, u32[]{:S(2)}, u32[]{:S(2)}) collective-permute-start(f32[4,256]{1,0:T(4,128)S(1)} %add_add_fusion), channel_id=1, source_target_pairs={{0,4},{4,8},{8,12},{12,0},{1,5},{5,9},{9,13},{13,1},{2,6},{6,10},{... | collective-permute-start | bytes 12296 | tf_op jit(solution)/shard_map/ppermute | solution.py:18
  189.5 16.7 %collective-permute-start.29 = (f32[4,256]{1,0:T(4,128)S(1)}, f32[4,256]{1,0:T(4,128)S(1)}, u32[]{:S(2)}, u32[]{:S(2)}) collective-permute-start(f32[4,256]{1,0:T(4,128)S(1)} %add_add_fusion), channel_id=1, source_target_pairs={{0,8},{4,12},{8,0},{12,4},{1,9},{5,13},{9,1},{13,5},{2,10},{6,14},... | collective-permute-start | bytes 12296 | tf_op jit(solution)/shard_map/ppermute | solution.py:18
  192.8 15.6 %collective-permute-start.28 = (bf16[256,384]{1,0:T(8,128)(2,1)S(1)}, bf16[256,384]{1,0:T(8,128)(2,1)S(1)}, u32[]{:S(2)}, u32[]{:S(2)}) collective-permute-start(bf16[256,384]{1,0:T(8,128)(2,1)S(1)} %get-tuple-element.115), channel_id=1, source_target_pairs={{0,19},{1,16},{2,17},{3,18},{16,35},{17,32},{18,33},{19,34},{32,51... | collective-permute-start | bytes 589832 | tf_op jit(solution)/shard_map/ppermute | solution.py:34
  194.7 14.4 %collective-permute-start.23 = (bf16[256,384]{1,0:T(8,128)(2,1)S(1)}, bf16[256,384]{1,0:T(8,128)(2,1)S(1)}, u32[]{:S(2)}, u32[]{:S(2)}) collective-permute-start(bf16[256,384]{1,0:T(8,128)(2,1)S(1)} %get-tuple-element.114), channel_id=1, source_target_pairs={{0,17},{1,18},{2,19},{3,16},{16,33},{17,34},{18,35},{19,32},{32,49... | collective-permute-start | bytes 589832 | tf_op jit(solution)/shard_map/ppermute | solution.py:34
  201.7 7.8 %collective-permute-start.22 = (bf16[256,384]{1,0:T(8,128)(2,1)S(1)}, bf16[256,384]{1,0:T(8,128)(2,1)S(1)}, u32[]{:S(2)}, u32[]{:S(2)}) collective-permute-start(bf16[256,384]{1,0:T(8,128)(2,1)S(1)} %fusion.4), channel_id=1, source_target_pairs={{0,16},{1,17},{2,18},{3,19},{16,32},{17,33},{18,34},{19,35},{32,48... | collective-permute-start | bytes 589832 | tf_op jit(solution)/shard_map/ppermute | solution.py:34
  206.5 7.0 %collective-permute-start.32 = (bf16[256,384]{1,0:T(8,128)(2,1)S(1)}, bf16[256,384]{1,0:T(8,128)(2,1)S(1)}, u32[]{:S(2)}, u32[]{:S(2)}) collective-permute-start(bf16[256,384]{1,0:T(8,128)(2,1)S(1)} %fusion), channel_id=1, source_target_pairs={{16,0},{32,16},{48,32},{64,48},{80,64},{96,80},{112,96},{128,112},... | collective-permute-start | bytes 589832 | tf_op jit(solution)/shard_map/ppermute | solution.py:24
where the time goes:
time: 215 us; the launch traced here: 214 us
  starting transfers between devices  81.3 us (38%)
  waiting for transfers between devices  50.7 us (24%)
  blocking collectives  34.1 us (16%)
  Pallas kernels  28.6 us (13%)
  other arithmetic  10.7 us (5%)
  local copies, waits for them, and re-layouts  7.58 us (4%)
    ppermute x27, starting transfers between devices, turned(): lax.ppermute(value, axis, [(i, (i + steps) % SIDE) for i in range(SIDE)])  41.7 us
    ppermute x27, waiting for transfers between devices, turned(): lax.ppermute(value, axis, [(i, (i + steps) % SIDE) for i in range(SIDE)])  37 us
    pallas_call x2, Pallas kernels, project(): pl.pallas_call(kernel, out_shape=[half] * 2 + [whole] * 3, in_specs=[pl.B...  25.5 us
    ppermute x4, starting transfers between devices, shifted_turned(): return lax.ppermute(value, ('pipe', 'z'), pairs)  20 us
    all_gather x1, blocking collectives, per_device(): near_up = lax.all_gather(upstream, 'z', axis=0)  18.7 us
    ppermute x1, starting transfers between devices, mirrored(): lax.ppermute(value, 'pipe', [(s, count - 1 - s) for s in range(count)])  17.7 us
    all_gather x1, blocking collectives, per_device(): near_tok = lax.all_gather(tokens_affine, 'z', axis=0)  15.4 us
    ppermute x4, waiting for transfers between devices, shifted_turned(): return lax.ppermute(value, ('pipe', 'z'), pairs)  10.6 us
  transfers between devices with their start and end apart: 33, of which 11 were waited for; matrix products, arithmetic and copies ran while one was open for 7% of the time, Pallas kernels for 13%

commit v1 on v0

--- a/solution.py
+++ b/solution.py
@@ -334,6 +334,7 @@
     by_left, by_right = turned(p1, "y", 1), turned(p3, "y", -1)
     by_left, by_right, r1, r2, r3 = ordered((by_left, by_right, r1, r2, r3))
     f0, f1, f2, f3 = three(p0, by_left, by_right)
+    r1, r2, r3, f2 = ordered((r1, r2, r3, f2))
     f0 = add(f0, tokens)
     s2, s1 = shifted_turned(f2, 2), shifted_turned(f1, 1)
     s3, s0 = shifted_turned(f3, -1), shifted_turned(f0, 0)
@@ -357,7 +358,7 @@
             jnp.sum(grad_scaled * stashed, axis=-1),
         ]
     )
-    sums, s2 = ordered((summed(sums, "z"), s2))
+    sums, s1, s2, s3 = ordered((summed(sums, "z"), s1, s2, s3))
     sums = summed(sums, "y") / full
     stash_mean, square_mean, grad_mean, cross_mean = (sums[i][:, None] for i in range(4))
     inv_std = lax.rsqrt(square_mean - stash_mean * stash_mean + norm_epsilon)

time: 215 us -> 215 us (level)
  starting transfers between devices: 81.3 us -> 78.9 us
    ppermute x4, starting transfers between devices: 20 us -> 17.8 us  [shifted_turned(): return lax.ppermute(value, ('pipe', 'z'), pairs)]
  transfers between devices with their start and end apart: 33 -> 33, of which waited for: 11 -> 11; matrix products, arithmetic and copies ran while one was open for 7% -> 6% of each run, Pallas kernels for 13% -> 13%
where the time goes in v1:
time: 215 us; the launch traced here: 214 us
  starting transfers between devices  78.9 us (37%)
  waiting for transfers between devices  52.2 us (24%)
  blocking collectives  34.1 us (16%)
  Pallas kernels  28.7 us (13%)
  other arithmetic  10.8 us (5%)
  local copies, waits for them, and re-layouts  7.55 us (4%)
    ppermute x27, starting transfers between devices, turned(): lax.ppermute(value, axis, [(i, (i + steps) % SIDE) for i in range(SIDE)])  41.5 us
    ppermute x27, waiting for transfers between devices, turned(): lax.ppermute(value, axis, [(i, (i + steps) % SIDE) for i in range(SIDE)])  37 us
    pallas_call x2, Pallas kernels, project(): pl.pallas_call(kernel, out_shape=[half] * 2 + [whole] * 3, in_specs=[pl.B...  25.5 us
    all_gather x1, blocking collectives, per_device(): near_up = lax.all_gather(upstream, 'z', axis=0)  18.7 us
    ppermute x4, starting transfers between devices, shifted_turned(): return lax.ppermute(value, ('pipe', 'z'), pairs)  17.8 us
    ppermute x1, starting transfers between devices, mirrored(): lax.ppermute(value, 'pipe', [(s, count - 1 - s) for s in range(count)])  17.7 us
    all_gather x1, blocking collectives, per_device(): near_tok = lax.all_gather(tokens_affine, 'z', axis=0)  15.4 us
    ppermute x4, waiting for transfers between devices, shifted_turned(): return lax.ppermute(value, ('pipe', 'z'), pairs)  11.3 us
  transfers between devices with their start and end apart: 33, of which 11 were waited for; matrix products, arithmetic and copies ran while one was open for 6% of the time, Pallas kernels for 13%

profile of v1, /device:TPU:75, one launch (start us, length us, event | category | flops | bytes accessed | tf_op | source)
XLA Modules:
  0.0 213.5 jit_solution(14439583585037229453)
XLA Ops:
  0.6 18.7 %all_gather.9.near = bf16[4,256,384]{2,1,0:T(8,128)(2,1)S(1)} all-gather(bf16[1,256,384]{2,1,0:T(8,128)(2,1)} %param.12), channel_id=1, replica_groups=mesh['pipe'=16,'y'=4,'z'=4] {'z'}, dimensions={0}, use_global_device_ids=true | all-gather | bytes 983040 | tf_op jit(solution)/shard_map/all_gather | solution.py:293
  19.3 0.2 collective-permute-start
  19.5 1.3 collective-permute-start.1
  20.9 1.1 maximum_maximum_fusion
  21.9 3.3 %collective-permute-start.2 = (bf16[272,384]{1,0:T(8,128)(2,1)S(1)}, bf16[272,384]{1,0:T(8,128)(2,1)S(1)}, u32[]{:S(2)}, u32[]{:S(2)}) collective-permute-start(bf16[272,384]{1,0:T(8,128)(2,1)S(1)} %maximum_maximum_fusion), channel_id=1, source_target_pairs={{0,8},{4,12},{8,0},{12,4},{1,9},{5,13},{9,1},{13,5},{2,10},{6,14},... | collective-permute-start | bytes 626696 | tf_op jit(solution)/shard_map/ppermute | solution.py:18
  25.2 15.4 %all-gather = bf16[1088,384]{1,0:T(8,128)(2,1)S(1)} all-gather(bf16[272,384]{1,0:T(8,128)(2,1)S(1)} %maximum_maximum_fusion), channel_id=2, replica_groups=mesh['pipe'=16,'y'=4,'z'=4] {'z'}, dimensions={0}, use_global_device_ids=true | all-gather | bytes 1044480 | tf_op jit(solution)/shard_map/all_gather | solution.py:296
  40.9 1.5 collective-permute-start.4
  42.4 3.2 %shard_map.122 = (bf16[3,256,256]{2,1,0:T(8,128)(2,1)}, bf16[3,256,256]{2,1,0:T(8,128)(2,1)}) custom-call(f32[3,256,256]{2,1,0:T(8,128)} %bitcast.64, f32[3,256,256]{2,1,0:T(8,128)} %bitcast.65), custom_call_target="tpu_custom_call" | custom-call | tf_op jit(solution)/shard_map/pallas_call | solution.py:301
  45.6 3.4 %collective-permute-done.3.fa = bf16[2,256,384]{2,1,0:T(8,128)(2,1)S(1)} collective-permute-done((bf16[2,256,384]{2,1,0:T(8,128)(2,1)S(1)}, bf16[2,256,384]{2,1,0:T(8,128)(2,1)S(1)}, u32[]{:S(2)}, u32[]{:S(2)}) %collective-permute-start.3) | collective-permute-done | bytes 393248 | tf_op jit(solution)/shard_map/ppermute | solution.py:18
  48.9 2.5 %collective-permute-start.8 = (bf16[4,272,384]{2,1,0:T(8,128)(2,1)S(1)}, bf16[4,272,384]{2,1,0:T(8,128)(2,1)S(1)}, u32[]{:S(2)}, u32[]{:S(2)}) collective-permute-start(bf16[4,272,384]{2,1,0:T(8,128)(2,1)S(1)} %bitcast.58), channel_id=1, source_target_pairs={{0,12},{4,0},{8,4},{12,8},{1,13},{5,1},{9,5},{13,9},{2,14},{6,2},{... | collective-permute-start | bytes 2506760 | tf_op jit(solution)/shard_map/ppermute | solution.py:18
  51.5 0.6 pad_add_fusion.place
  52.1 1.5 collective-permute-start.5
  53.6 3.2 %collective-permute-start.6 = (bf16[272,384]{1,0:T(8,128)(2,1)S(1)}, bf16[272,384]{1,0:T(8,128)(2,1)S(1)}, u32[]{:S(2)}, u32[]{:S(2)}) collective-permute-start(bf16[272,384]{1,0:T(8,128)(2,1)S(1)} %collective-permute-done.2.fa), channel_id=1, source_target_pairs={{0,2},{1,3},{2,0},{3,1},{4,6},{5,7},{6,4},{7,5},{8,10},{9,11},{10,... | collective-permute-start | bytes 626696 | tf_op jit(solution)/shard_map/ppermute | solution.py:18
  56.8 1.5 collective-permute-start.7
  58.3 11.7 %shard_map.123 = (bf16[2,256,384]{2,1,0:T(8,128)(2,1)}, bf16[2,256,384]{2,1,0:T(8,128)(2,1)}, bf16[4,256,384]{2,1,0:T(8,128)(2,1)}, bf16[4,256,384]{2,1,0:T(8,128)(2,1)}, bf16[4,256,384]{2,1,0:T(8,128)(2,1)}) custom-call(s32[2]{0:T(128)} %pad_add_fusion.place, bf16[4,256,384]{2,1,0:T(8,128)(2,1)} %copy-done.1, bf16[4,256,384]{2,1,0:T(8,128)(2,1)} %copy-done.2, ...), custom_call_target="tpu_custom_call" | custom-call | flops 2516582400 | bytes 15728640 | tf_op jit(solution)/shard_map/pallas_call | solution.py:221
  70.1 0.1 collective-permute-start.10
  70.2 1.5 collective-permute-start.11
  71.7 1.0 slice.51
  72.7 1.0 slice.52
  73.8 6.9 %collective-permute-done.10 = bf16[2,256,384]{2,1,0:T(8,128)(2,1)S(1)} collective-permute-done((bf16[2,256,384]{2,1,0:T(8,128)(2,1)}, bf16[2,256,384]{2,1,0:T(8,128)(2,1)S(1)}, u32[]{:S(2)}, u32[]{:S(2)}) %collective-permute-start.10) | collective-permute-done | bytes 393248 | tf_op jit(solution)/shard_map/ppermute | solution.py:18
  80.7 0.1 add_convert_fusion.5
  81.2 0.4 copy-done.4
  81.6 0.3 copy-done.5
  82.0 3.0 %collective-permute-start.13 = (bf16[4,256,384]{2,1,0:T(8,128)(2,1)S(1)}, bf16[4,256,384]{2,1,0:T(8,128)(2,1)S(1)}, u32[]{:S(2)}, u32[]{:S(2)}) collective-permute-start(bf16[4,256,384]{2,1,0:T(8,128)(2,1)S(1)} %pad_maximum_fusion.1), channel_id=1, source_target_pairs={{0,12},{4,0},{8,4},{12,8},{1,13},{5,1},{9,5},{13,9},{2,14},{6,2},{... | collective-permute-start | bytes 2359304 | tf_op jit(solution)/shard_map/ppermute | solution.py:18
  85.0 0.1 maximum_maximum_fusion.1
  85.1 17.7 %collective-permute-start.14 = (bf16[272,384]{1,0:T(8,128)(2,1)S(1)}, bf16[272,384]{1,0:T(8,128)(2,1)S(1)}, u32[]{:S(2)}, u32[]{:S(2)}) collective-permute-start(bf16[272,384]{1,0:T(8,128)(2,1)S(1)} %maximum_maximum_fusion.1), channel_id=1, source_target_pairs={{0,240},{16,224},{32,208},{48,192},{64,176},{80,160},{96,144},{112... | collective-permute-start | bytes 626696 | tf_op jit(solution)/shard_map/ppermute | solution.py:39
  102.8 2.0 pad_maximum_fusion.4.fb
  104.8 13.8 %shard_map.124 = (bf16[2,256,384]{2,1,0:T(8,128)(2,1)}, bf16[2,256,384]{2,1,0:T(8,128)(2,1)}, bf16[4,256,384]{2,1,0:T(8,128)(2,1)}, bf16[4,256,384]{2,1,0:T(8,128)(2,1)}, bf16[4,256,384]{2,1,0:T(8,128)(2,1)}) custom-call(s32[2]{0:T(128)} %pad_add_fusion.place, bf16[4,272,384]{2,1,0:T(8,128)(2,1)} %bitcast.60, bf16[4,272,384]{2,1,0:T(8,128)(2,1)} %copy-done.4, ...), custom_call_target="tpu_custom_call" | custom-call | flops 2516582400 | bytes 15728640 | tf_op jit(solution)/shard_map/pallas_call | solution.py:221
  118.7 0.6 copy-done.21
  119.3 1.7 collective-permute-start.15
  121.0 0.6 collective-permute-start.16
  121.6 1.0 slice.55
  122.7 1.0 slice.56
  123.7 7.6 %collective-permute-done.15 = bf16[2,256,384]{2,1,0:T(8,128)(2,1)S(1)} collective-permute-done((bf16[2,256,384]{2,1,0:T(8,128)(2,1)}, bf16[2,256,384]{2,1,0:T(8,128)(2,1)S(1)}, u32[]{:S(2)}, u32[]{:S(2)}) %collective-permute-start.15) | collective-permute-done | bytes 393248 | tf_op jit(solution)/shard_map/ppermute | solution.py:18
  131.3 1.0 collective-permute-done.16
  132.6 1.0 collective-permute-start.17
  133.8 0.8 collective-permute-start.18
  134.7 1.7 add_convert_fusion.1
  136.4 0.8 slice_bitcast_fusion.5
  137.2 2.5 %collective-permute-start.20 = (bf16[256,384]{1,0:T(8,128)(2,1)}, bf16[256,384]{1,0:T(8,128)(2,1)}, u32[]{:S(2)}, u32[]{:S(2)}) collective-permute-start(bf16[256,384]{1,0:T(8,128)(2,1)} %get-tuple-element.130), channel_id=1, source_target_pairs={{0,2},{1,3},{2,0},{3,1},{4,6},{5,7},{6,4},{7,5},{8,10},{9,11},{10,... | collective-permute-start | bytes 589832 | tf_op jit(solution)/shard_map/ppermute | solution.py:18
  139.7 2.4 %collective-permute-start.21 = (bf16[256,384]{1,0:T(8,128)(2,1)}, bf16[256,384]{1,0:T(8,128)(2,1)}, u32[]{:S(2)}, u32[]{:S(2)}) collective-permute-start(bf16[256,384]{1,0:T(8,128)(2,1)} %get-tuple-element.129), channel_id=1, source_target_pairs={{0,3},{1,0},{2,1},{3,2},{4,7},{5,4},{6,5},{7,6},{8,11},{9,8},{10,9... | collective-permute-start | bytes 589832 | tf_op jit(solution)/shard_map/ppermute | solution.py:18
  142.1 0.2 copy.15
  142.3 6.3 %collective-permute-done.19 = bf16[256,384]{1,0:T(8,128)(2,1)} collective-permute-done((bf16[256,384]{1,0:T(8,128)(2,1)}, bf16[256,384]{1,0:T(8,128)(2,1)}, u32[]{:S(2)}, u32[]{:S(2)}) %collective-permute-start.19) | collective-permute-done | bytes 196640 | tf_op jit(solution)/shard_map/ppermute | solution.py:18
  148.6 6.0 %collective-permute-done.20 = bf16[256,384]{1,0:T(8,128)(2,1)} collective-permute-done((bf16[256,384]{1,0:T(8,128)(2,1)}, bf16[256,384]{1,0:T(8,128)(2,1)}, u32[]{:S(2)}, u32[]{:S(2)}) %collective-permute-start.20) | collective-permute-done | bytes 196640 | tf_op jit(solution)/shard_map/ppermute | solution.py:18
  154.6 5.8 %collective-permute-done.21 = bf16[256,384]{1,0:T(8,128)(2,1)} collective-permute-done((bf16[256,384]{1,0:T(8,128)(2,1)}, bf16[256,384]{1,0:T(8,128)(2,1)}, u32[]{:S(2)}, u32[]{:S(2)}) %collective-permute-start.21) | collective-permute-done | bytes 196640 | tf_op jit(solution)/shard_map/ppermute | solution.py:18
  160.4 1.9 add_convert_fusion
  162.4 1.6 fusion.6
  164.0 1.4 collective-permute-start.25
  165.4 2.3 %collective-permute-start.24 = (f32[4,256]{1,0:T(4,128)S(1)}, f32[4,256]{1,0:T(4,128)S(1)}, u32[]{:S(2)}, u32[]{:S(2)}) collective-permute-start(f32[4,256]{1,0:T(4,128)S(1)} %pad_maximum_fusion.5), channel_id=1, source_target_pairs={{0,1},{1,2},{2,3},{3,0},{4,5},{5,6},{6,7},{7,4},{8,9},{9,10},{10,1... | collective-permute-start | bytes 12296 | tf_op jit(solution)/shard_map/ppermute | solution.py:18
  167.6 3.0 %collective-permute-start.23 = (f32[4,256]{1,0:T(4,128)S(1)}, f32[4,256]{1,0:T(4,128)S(1)}, u32[]{:S(2)}, u32[]{:S(2)}) collective-permute-start(f32[4,256]{1,0:T(4,128)S(1)} %pad_maximum_fusion.5), channel_id=1, source_target_pairs={{0,2},{1,3},{2,0},{3,1},{4,6},{5,7},{6,4},{7,5},{8,10},{9,11},{10,... | collective-permute-start | bytes 12296 | tf_op jit(solution)/shard_map/ppermute | solution.py:18
  170.6 3.6 %collective-permute-start.26 = (bf16[256,384]{1,0:T(8,128)(2,1)S(1)}, bf16[256,384]{1,0:T(8,128)(2,1)S(1)}, u32[]{:S(2)}, u32[]{:S(2)}) collective-permute-start(bf16[256,384]{1,0:T(8,128)(2,1)S(1)} %get-tuple-element.127), channel_id=1, source_target_pairs={{0,17},{1,18},{2,19},{3,16},{16,33},{17,34},{18,35},{19,32},{32,49... | collective-permute-start | bytes 589832 | tf_op jit(solution)/shard_map/ppermute | solution.py:34
  174.3 4.7 %collective-permute-start.27 = (bf16[256,384]{1,0:T(8,128)(2,1)S(1)}, bf16[256,384]{1,0:T(8,128)(2,1)S(1)}, u32[]{:S(2)}, u32[]{:S(2)}) collective-permute-start(bf16[256,384]{1,0:T(8,128)(2,1)S(1)} %get-tuple-element.115), channel_id=1, source_target_pairs={{0,18},{1,19},{2,16},{3,17},{16,34},{17,35},{18,32},{19,33},{32,50... | collective-permute-start | bytes 589832 | tf_op jit(solution)/shard_map/ppermute | solution.py:34
  179.0 5.2 %collective-permute-start.28 = (bf16[256,384]{1,0:T(8,128)(2,1)S(1)}, bf16[256,384]{1,0:T(8,128)(2,1)S(1)}, u32[]{:S(2)}, u32[]{:S(2)}) collective-permute-start(bf16[256,384]{1,0:T(8,128)(2,1)S(1)} %get-tuple-element.126), channel_id=1, source_target_pairs={{0,19},{1,16},{2,17},{3,18},{16,35},{17,32},{18,33},{19,34},{32,51... | collective-permute-start | bytes 589832 | tf_op jit(solution)/shard_map/ppermute | solution.py:34
  184.2 6.7 %collective-permute-done.27 = bf16[256,384]{1,0:T(8,128)(2,1)S(1)} collective-permute-done((bf16[256,384]{1,0:T(8,128)(2,1)S(1)}, bf16[256,384]{1,0:T(8,128)(2,1)S(1)}, u32[]{:S(2)}, u32[]{:S(2)}) %collective-permute-start.27) | collective-permute-done | bytes 196640 | tf_op jit(solution)/shard_map/ppermute | solution.py:34
  190.9 4.2 %collective-permute-done.28 = bf16[256,384]{1,0:T(8,128)(2,1)S(1)} collective-permute-done((bf16[256,384]{1,0:T(8,128)(2,1)S(1)}, bf16[256,384]{1,0:T(8,128)(2,1)S(1)}, u32[]{:S(2)}, u32[]{:S(2)}) %collective-permute-start.28) | collective-permute-done | bytes 196640 | tf_op jit(solution)/shard_map/ppermute | solution.py:34
  195.2 2.9 %collective-permute-start.31 = (f32[4,256]{1,0:T(4,128)S(1)}, f32[4,256]{1,0:T(4,128)S(1)}, u32[]{:S(2)}, u32[]{:S(2)}) collective-permute-start(f32[4,256]{1,0:T(4,128)S(1)} %add_add_fusion), channel_id=1, source_target_pairs={{0,12},{4,0},{8,4},{12,8},{1,13},{5,1},{9,5},{13,9},{2,14},{6,2},{... | collective-permute-start | bytes 12296 | tf_op jit(solution)/shard_map/ppermute | solution.py:18
  198.1 3.1 %collective-permute-start.29 = (f32[4,256]{1,0:T(4,128)S(1)}, f32[4,256]{1,0:T(4,128)S(1)}, u32[]{:S(2)}, u32[]{:S(2)}) collective-permute-start(f32[4,256]{1,0:T(4,128)S(1)} %add_add_fusion), channel_id=1, source_target_pairs={{0,8},{4,12},{8,0},{12,4},{1,9},{5,13},{9,1},{13,5},{2,10},{6,14},... | collective-permute-start | bytes 12296 | tf_op jit(solution)/shard_map/ppermute | solution.py:18
  201.3 4.3 %collective-permute-start.22 = (bf16[256,384]{1,0:T(8,128)(2,1)S(1)}, bf16[256,384]{1,0:T(8,128)(2,1)S(1)}, u32[]{:S(2)}, u32[]{:S(2)}) collective-permute-start(bf16[256,384]{1,0:T(8,128)(2,1)S(1)} %fusion.4), channel_id=1, source_target_pairs={{0,16},{1,17},{2,18},{3,19},{16,32},{17,33},{18,34},{19,35},{32,48... | collective-permute-start | bytes 589832 | tf_op jit(solution)/shard_map/ppermute | solution.py:34
  205.6 0.2 fusion
  205.8 1.9 collective-permute-start.32
  207.8 0.4 collective-permute-done.22
  208.1 0.8 fusion.5
  208.9 3.9 %collective-permute-done.32 = bf16[256,384]{1,0:T(8,128)(2,1)S(1)} collective-permute-done((bf16[256,384]{1,0:T(8,128)(2,1)S(1)}, bf16[256,384]{1,0:T(8,128)(2,1)S(1)}, u32[]{:S(2)}, u32[]{:S(2)}) %collective-permute-start.32) | collective-permute-done | bytes 196640 | tf_op jit(solution)/shard_map/ppermute | solution.py:24
  212.8 0.7 copy.17
  (102 shorter events, 1.5 us)
Async XLA Ops:
  19.3 26.3 %copy-start.1 = (bf16[4,256,384]{2,1,0:T(8,128)(2,1)}, bf16[4,256,384]{2,1,0:T(8,128)(2,1)S(1)}, u32[]{:S(2)}) copy-start(bf16[4,256,384]{2,1,0:T(8,128)(2,1)S(1)} %all_gather.9.near) | copy-start | bytes 2359300
  19.3 21.3 %collective-permute-start = (bf16[4,256,384]{2,1,0:T(8,128)(2,1)S(1)}, bf16[4,256,384]{2,1,0:T(8,128)(2,1)S(1)}, u32[]{:S(2)}, u32[]{:S(2)}) collective-permute-start(bf16[4,256,384]{2,1,0:T(8,128)(2,1)S(1)} %all_gather.9.near), channel_id=1, source_target_pairs={{0,12},{4,0},{8,4},{12,8},{1,13},{5,1},{9,5},{13,9},{2,14},{6,2},{... | collective-permute-start | bytes 2359304 | tf_op jit(solution)/shard_map/ppermute | solution.py:18
  19.5 21.2 %collective-permute-start.1 = (bf16[4,256,384]{2,1,0:T(8,128)(2,1)S(1)}, bf16[4,256,384]{2,1,0:T(8,128)(2,1)S(1)}, u32[]{:S(2)}, u32[]{:S(2)}) collective-permute-start(bf16[4,256,384]{2,1,0:T(8,128)(2,1)S(1)} %all_gather.9.near), channel_id=1, source_target_pairs={{0,4},{4,8},{8,12},{12,0},{1,5},{5,9},{9,13},{13,1},{2,6},{6,10},{... | collective-permute-start | bytes 2359304 | tf_op jit(solution)/shard_map/ppermute | solution.py:18
  21.9 18.7 %collective-permute-start.2 = (bf16[272,384]{1,0:T(8,128)(2,1)S(1)}, bf16[272,384]{1,0:T(8,128)(2,1)S(1)}, u32[]{:S(2)}, u32[]{:S(2)}) collective-permute-start(bf16[272,384]{1,0:T(8,128)(2,1)S(1)} %maximum_maximum_fusion), channel_id=1, source_target_pairs={{0,8},{4,12},{8,0},{12,4},{1,9},{5,13},{9,1},{13,5},{2,10},{6,14},... | collective-permute-start | bytes 626696 | tf_op jit(solution)/shard_map/ppermute | solution.py:18
  40.6 10.8 %copy-start = (bf16[1088,384]{1,0:T(8,128)(2,1)}, bf16[1088,384]{1,0:T(8,128)(2,1)S(1)}, u32[]{:S(2)}) copy-start(bf16[1088,384]{1,0:T(8,128)(2,1)S(1)} %all-gather) | copy-start | bytes 2506756
  40.6 16.2 %copy-start.20 = (bf16[272,384]{1,0:T(8,128)(2,1)}, bf16[272,384]{1,0:T(8,128)(2,1)S(1)}, u32[]{:S(2)}) copy-start(bf16[272,384]{1,0:T(8,128)(2,1)S(1)} %collective-permute-done.2.fa) | copy-start | bytes 626692
  40.6 4.9 %copy-start.2 = (bf16[4,256,384]{2,1,0:T(8,128)(2,1)}, bf16[4,256,384]{2,1,0:T(8,128)(2,1)S(1)}, u32[]{:S(2)}) copy-start(bf16[4,256,384]{2,1,0:T(8,128)(2,1)S(1)} %collective-permute-done.right) | copy-start | bytes 2359300
  40.7 4.9 %copy-start.3 = (bf16[4,256,384]{2,1,0:T(8,128)(2,1)}, bf16[4,256,384]{2,1,0:T(8,128)(2,1)S(1)}, u32[]{:S(2)}) copy-start(bf16[4,256,384]{2,1,0:T(8,128)(2,1)S(1)} %collective-permute-done.1.left) | copy-start | bytes 2359300
  40.7 8.2 %collective-permute-start.3 = (bf16[2,256,384]{2,1,0:T(8,128)(2,1)S(1)}, bf16[2,256,384]{2,1,0:T(8,128)(2,1)S(1)}, u32[]{:S(2)}, u32[]{:S(2)}) collective-permute-start(bf16[2,256,384]{2,1,0:T(8,128)(2,1)S(1)} %slice.48), channel_id=1, source_target_pairs={{0,4},{4,8},{8,12},{12,0},{1,5},{5,9},{9,13},{13,1},{2,6},{6,10},{... | collective-permute-start | bytes 1179656 | tf_op jit(solution)/shard_map/ppermute | solution.py:18
  40.9 8.1 %collective-permute-start.4 = (bf16[2,256,384]{2,1,0:T(8,128)(2,1)S(1)}, bf16[2,256,384]{2,1,0:T(8,128)(2,1)S(1)}, u32[]{:S(2)}, u32[]{:S(2)}) collective-permute-start(bf16[2,256,384]{2,1,0:T(8,128)(2,1)S(1)} %slice.49), channel_id=1, source_target_pairs={{0,12},{4,0},{8,4},{12,8},{1,13},{5,1},{9,5},{13,9},{2,14},{6,2},{... | collective-permute-start | bytes 1179656 | tf_op jit(solution)/shard_map/ppermute | solution.py:18
  48.9 2.5 %copy-start.15 = (bf16[2,256,384]{2,1,0:T(8,128)(2,1)}, bf16[2,256,384]{2,1,0:T(8,128)(2,1)S(1)}, u32[]{:S(2)}) copy-start(bf16[2,256,384]{2,1,0:T(8,128)(2,1)S(1)} %collective-permute-done.3.fa) | copy-start | bytes 1179652
  48.9 2.5 %copy-start.16 = (bf16[2,256,384]{2,1,0:T(8,128)(2,1)}, bf16[2,256,384]{2,1,0:T(8,128)(2,1)S(1)}, u32[]{:S(2)}) copy-start(bf16[2,256,384]{2,1,0:T(8,128)(2,1)S(1)} %collective-permute-done.4.fb) | copy-start | bytes 1179652
  48.9 31.7 %collective-permute-start.8 = (bf16[4,272,384]{2,1,0:T(8,128)(2,1)S(1)}, bf16[4,272,384]{2,1,0:T(8,128)(2,1)S(1)}, u32[]{:S(2)}, u32[]{:S(2)}) collective-permute-start(bf16[4,272,384]{2,1,0:T(8,128)(2,1)S(1)} %bitcast.58), channel_id=1, source_target_pairs={{0,12},{4,0},{8,4},{12,8},{1,13},{5,1},{9,5},{13,9},{2,14},{6,2},{... | collective-permute-start | bytes 2506760 | tf_op jit(solution)/shard_map/ppermute | solution.py:18
  51.5 29.2 %collective-permute-start.9 = (bf16[4,272,384]{2,1,0:T(8,128)(2,1)S(1)}, bf16[4,272,384]{2,1,0:T(8,128)(2,1)S(1)}, u32[]{:S(2)}, u32[]{:S(2)}) collective-permute-start(bf16[4,272,384]{2,1,0:T(8,128)(2,1)S(1)} %bitcast.59), channel_id=1, source_target_pairs={{0,4},{4,8},{8,12},{12,0},{1,5},{5,9},{9,13},{13,1},{2,6},{6,10},{... | collective-permute-start | bytes 2506760 | tf_op jit(solution)/shard_map/ppermute | solution.py:18
  52.1 17.9 %collective-permute-start.5 = (bf16[272,384]{1,0:T(8,128)(2,1)S(1)}, bf16[272,384]{1,0:T(8,128)(2,1)S(1)}, u32[]{:S(2)}, u32[]{:S(2)}) collective-permute-start(bf16[272,384]{1,0:T(8,128)(2,1)S(1)} %collective-permute-done.2.fa), channel_id=1, source_target_pairs={{0,3},{1,0},{2,1},{3,2},{4,7},{5,4},{6,5},{7,6},{8,11},{9,8},{10,9... | collective-permute-start | bytes 626696 | tf_op jit(solution)/shard_map/ppermute | solution.py:18
  53.6 16.5 %collective-permute-start.6 = (bf16[272,384]{1,0:T(8,128)(2,1)S(1)}, bf16[272,384]{1,0:T(8,128)(2,1)S(1)}, u32[]{:S(2)}, u32[]{:S(2)}) collective-permute-start(bf16[272,384]{1,0:T(8,128)(2,1)S(1)} %collective-permute-done.2.fa), channel_id=1, source_target_pairs={{0,2},{1,3},{2,0},{3,1},{4,6},{5,7},{6,4},{7,5},{8,10},{9,11},{10,... | collective-permute-start | bytes 626696 | tf_op jit(solution)/shard_map/ppermute | solution.py:18
  56.8 13.3 %collective-permute-start.7 = (bf16[272,384]{1,0:T(8,128)(2,1)S(1)}, bf16[272,384]{1,0:T(8,128)(2,1)S(1)}, u32[]{:S(2)}, u32[]{:S(2)}) collective-permute-start(bf16[272,384]{1,0:T(8,128)(2,1)S(1)} %collective-permute-done.2.fa), channel_id=1, source_target_pairs={{0,1},{1,2},{2,3},{3,0},{4,5},{5,6},{6,7},{7,4},{8,9},{9,10},{10,1... | collective-permute-start | bytes 626696 | tf_op jit(solution)/shard_map/ppermute | solution.py:18
  70.0 10.7 %copy-start.10 = (bf16[4,256,384]{2,1,0:T(8,128)(2,1)S(1)}, bf16[4,256,384]{2,1,0:T(8,128)(2,1)}, u32[]{:S(2)}) copy-start(bf16[4,256,384]{2,1,0:T(8,128)(2,1)} %get-tuple-element.74) | copy-start | bytes 2359300
  70.0 11.9 %copy-start.17 = (bf16[272,384]{1,0:T(8,128)(2,1)}, bf16[272,384]{1,0:T(8,128)(2,1)S(1)}, u32[]{:S(2)}) copy-start(bf16[272,384]{1,0:T(8,128)(2,1)S(1)} %collective-permute-done.5) | copy-start | bytes 626692
  70.0 11.9 %copy-start.18 = (bf16[272,384]{1,0:T(8,128)(2,1)}, bf16[272,384]{1,0:T(8,128)(2,1)S(1)}, u32[]{:S(2)}) copy-start(bf16[272,384]{1,0:T(8,128)(2,1)S(1)} %collective-permute-done.6) | copy-start | bytes 626692
  70.1 10.9 %copy-start.19 = (bf16[272,384]{1,0:T(8,128)(2,1)}, bf16[272,384]{1,0:T(8,128)(2,1)S(1)}, u32[]{:S(2)}) copy-start(bf16[272,384]{1,0:T(8,128)(2,1)S(1)} %collective-permute-done.7) | copy-start | bytes 626692
  70.1 10.6 %collective-permute-start.10 = (bf16[2,256,384]{2,1,0:T(8,128)(2,1)}, bf16[2,256,384]{2,1,0:T(8,128)(2,1)S(1)}, u32[]{:S(2)}, u32[]{:S(2)}) collective-permute-start(bf16[2,256,384]{2,1,0:T(8,128)(2,1)} %get-tuple-element.76), channel_id=1, source_target_pairs={{0,4},{4,8},{8,12},{12,0},{1,5},{5,9},{9,13},{13,1},{2,6},{6,10},{... | collective-permute-start | bytes 1179656 | tf_op jit(solution)/shard_map/ppermute | solution.py:18
  70.2 10.5 %collective-permute-start.11 = (bf16[2,256,384]{2,1,0:T(8,128)(2,1)}, bf16[2,256,384]{2,1,0:T(8,128)(2,1)S(1)}, u32[]{:S(2)}, u32[]{:S(2)}) collective-permute-start(bf16[2,256,384]{2,1,0:T(8,128)(2,1)} %get-tuple-element.77), channel_id=1, source_target_pairs={{0,12},{4,0},{8,4},{12,8},{1,13},{5,1},{9,5},{13,9},{2,14},{6,2},{... | collective-permute-start | bytes 1179656 | tf_op jit(solution)/shard_map/ppermute | solution.py:18
  73.8 7.3 %copy-start.8 = (bf16[4,256,384]{2,1,0:T(8,128)(2,1)S(1)}, bf16[4,256,384]{2,1,0:T(8,128)(2,1)}, u32[]{:S(2)}) copy-start(bf16[4,256,384]{2,1,0:T(8,128)(2,1)} %get-tuple-element.79) | copy-start | bytes 2359300
  80.7 0.9 copy-start.4
  80.7 1.2 copy-start.5
  80.9 4.1 %copy-start.23 = (bf16[1,3,256]{2,1,0:T(4,128)(2,1)S(1)}, bf16[1,3,256]{2,1,0:T(4,128)(2,1)}, u32[]{:S(2)}) copy-start(bf16[1,3,256]{2,1,0:T(4,128)(2,1)} %param.20) | copy-start | bytes 4612
  80.9 4.1 %copy-start.6 = (bf16[1,256,384]{2,1,0:T(8,128)(2,1)S(1)}, bf16[1,256,384]{2,1,0:T(8,128)(2,1)}, u32[]{:S(2)}) copy-start(bf16[1,256,384]{2,1,0:T(8,128)(2,1)} %param.19) | copy-start | bytes 589828
  80.9 37.7 %collective-permute-start.12 = (bf16[4,256,384]{2,1,0:T(8,128)(2,1)S(1)}, bf16[4,256,384]{2,1,0:T(8,128)(2,1)}, u32[]{:S(2)}, u32[]{:S(2)}) collective-permute-start(bf16[4,256,384]{2,1,0:T(8,128)(2,1)S(1)} %pad_maximum_fusion), channel_id=1, source_target_pairs={{0,4},{4,8},{8,12},{12,0},{1,5},{5,9},{9,13},{13,1},{2,6},{6,10},{... | collective-permute-start | bytes 2359304 | tf_op jit(solution)/shard_map/ppermute | solution.py:18
  82.0 36.7 %collective-permute-start.13 = (bf16[4,256,384]{2,1,0:T(8,128)(2,1)S(1)}, bf16[4,256,384]{2,1,0:T(8,128)(2,1)S(1)}, u32[]{:S(2)}, u32[]{:S(2)}) collective-permute-start(bf16[4,256,384]{2,1,0:T(8,128)(2,1)S(1)} %pad_maximum_fusion.1), channel_id=1, source_target_pairs={{0,12},{4,0},{8,4},{12,8},{1,13},{5,1},{9,5},{13,9},{2,14},{6,2},{... | collective-permute-start | bytes 2359304 | tf_op jit(solution)/shard_map/ppermute | solution.py:18
  85.1 33.5 %collective-permute-start.14 = (bf16[272,384]{1,0:T(8,128)(2,1)S(1)}, bf16[272,384]{1,0:T(8,128)(2,1)S(1)}, u32[]{:S(2)}, u32[]{:S(2)}) collective-permute-start(bf16[272,384]{1,0:T(8,128)(2,1)S(1)} %maximum_maximum_fusion.1), channel_id=1, source_target_pairs={{0,240},{16,224},{32,208},{48,192},{64,176},{80,160},{96,144},{112... | collective-permute-start | bytes 626696 | tf_op jit(solution)/shard_map/ppermute | solution.py:39
  104.8 16.8 %copy-start.24 = (bf16[1,384]{1,0:T(2,128)(2,1)S(1)}, bf16[1,384]{1,0:T(2,128)(2,1)}, u32[]{:S(2)}) copy-start(bf16[1,384]{1,0:T(2,128)(2,1)} %param.13) | copy-start | bytes 2308
  118.6 13.7 %copy-start.9 = (bf16[4,256,384]{2,1,0:T(8,128)(2,1)S(1)}, bf16[4,256,384]{2,1,0:T(8,128)(2,1)}, u32[]{:S(2)}) copy-start(bf16[4,256,384]{2,1,0:T(8,128)(2,1)} %get-tuple-element.95) | copy-start | bytes 2359300
  118.6 0.7 copy-start.21
  118.6 13.7 %copy-start.13 = (bf16[4,256,384]{2,1,0:T(8,128)(2,1)}, bf16[4,256,384]{2,1,0:T(8,128)(2,1)S(1)}, u32[]{:S(2)}) copy-start(bf16[4,256,384]{2,1,0:T(8,128)(2,1)S(1)} %collective-permute-done.13) | copy-start | bytes 2359300
  119.3 12.0 %collective-permute-start.15 = (bf16[2,256,384]{2,1,0:T(8,128)(2,1)}, bf16[2,256,384]{2,1,0:T(8,128)(2,1)S(1)}, u32[]{:S(2)}, u32[]{:S(2)}) collective-permute-start(bf16[2,256,384]{2,1,0:T(8,128)(2,1)} %get-tuple-element.98), channel_id=1, source_target_pairs={{0,4},{4,8},{8,12},{12,0},{1,5},{5,9},{9,13},{13,1},{2,6},{6,10},{... | collective-permute-start | bytes 1179656 | tf_op jit(solution)/shard_map/ppermute | solution.py:18
  121.0 11.3 %collective-permute-start.16 = (bf16[2,256,384]{2,1,0:T(8,128)(2,1)}, bf16[2,256,384]{2,1,0:T(8,128)(2,1)S(1)}, u32[]{:S(2)}, u32[]{:S(2)}) collective-permute-start(bf16[2,256,384]{2,1,0:T(8,128)(2,1)} %get-tuple-element.99), channel_id=1, source_target_pairs={{0,12},{4,0},{8,4},{12,8},{1,13},{5,1},{9,5},{13,9},{2,14},{6,2},{... | collective-permute-start | bytes 1179656 | tf_op jit(solution)/shard_map/ppermute | solution.py:18
  123.7 9.9 %copy-start.7 = (bf16[4,256,384]{2,1,0:T(8,128)(2,1)S(1)}, bf16[4,256,384]{2,1,0:T(8,128)(2,1)}, u32[]{:S(2)}) copy-start(bf16[4,256,384]{2,1,0:T(8,128)(2,1)} %get-tuple-element.101) | copy-start | bytes 2359300
  132.5 2.1 copy-start.25
  132.6 2.1 slice-start
  132.6 2.1 %copy-start.12 = (bf16[4,256,384]{2,1,0:T(8,128)(2,1)S(1)}, bf16[4,256,384]{2,1,0:T(8,128)(2,1)}, u32[]{:S(2)}) copy-start(bf16[4,256,384]{2,1,0:T(8,128)(2,1)} %get-tuple-element.103) | copy-start | bytes 2359300
  132.6 27.8 %collective-permute-start.17 = (bf16[4,256,384]{2,1,0:T(8,128)(2,1)S(1)}, bf16[4,256,384]{2,1,0:T(8,128)(2,1)}, u32[]{:S(2)}, u32[]{:S(2)}) collective-permute-start(bf16[4,256,384]{2,1,0:T(8,128)(2,1)S(1)} %pad_maximum_fusion.2), channel_id=1, source_target_pairs={{0,4},{4,8},{8,12},{12,0},{1,5},{5,9},{9,13},{13,1},{2,6},{6,10},{... | collective-permute-start | bytes 2359304 | tf_op jit(solution)/shard_map/ppermute | solution.py:18
  133.8 26.6 %collective-permute-start.18 = (bf16[4,256,384]{2,1,0:T(8,128)(2,1)S(1)}, bf16[4,256,384]{2,1,0:T(8,128)(2,1)}, u32[]{:S(2)}, u32[]{:S(2)}) collective-permute-start(bf16[4,256,384]{2,1,0:T(8,128)(2,1)S(1)} %pad_maximum_fusion.3), channel_id=1, source_target_pairs={{0,12},{4,0},{8,4},{12,8},{1,13},{5,1},{9,5},{13,9},{2,14},{6,2},{... | collective-permute-start | bytes 2359304 | tf_op jit(solution)/shard_map/ppermute | solution.py:18
  137.2 11.4 %collective-permute-start.19 = (bf16[256,384]{1,0:T(8,128)(2,1)}, bf16[256,384]{1,0:T(8,128)(2,1)}, u32[]{:S(2)}, u32[]{:S(2)}) collective-permute-start(bf16[256,384]{1,0:T(8,128)(2,1)} %get-tuple-element.131), channel_id=1, source_target_pairs={{0,1},{1,2},{2,3},{3,0},{4,5},{5,6},{6,7},{7,4},{8,9},{9,10},{10,1... | collective-permute-start | bytes 589832 | tf_op jit(solution)/shard_map/ppermute | solution.py:18
  137.2 17.4 %collective-permute-start.20 = (bf16[256,384]{1,0:T(8,128)(2,1)}, bf16[256,384]{1,0:T(8,128)(2,1)}, u32[]{:S(2)}, u32[]{:S(2)}) collective-permute-start(bf16[256,384]{1,0:T(8,128)(2,1)} %get-tuple-element.130), channel_id=1, source_target_pairs={{0,2},{1,3},{2,0},{3,1},{4,6},{5,7},{6,4},{7,5},{8,10},{9,11},{10,... | collective-permute-start | bytes 589832 | tf_op jit(solution)/shard_map/ppermute | solution.py:18
  139.7 20.7 %collective-permute-start.21 = (bf16[256,384]{1,0:T(8,128)(2,1)}, bf16[256,384]{1,0:T(8,128)(2,1)}, u32[]{:S(2)}, u32[]{:S(2)}) collective-permute-start(bf16[256,384]{1,0:T(8,128)(2,1)} %get-tuple-element.129), channel_id=1, source_target_pairs={{0,3},{1,0},{2,1},{3,2},{4,7},{5,4},{6,5},{7,6},{8,11},{9,8},{10,9... | collective-permute-start | bytes 589832 | tf_op jit(solution)/shard_map/ppermute | solution.py:18
  142.3 20.1 %copy-start.22 = (bf16[272,384]{1,0:T(8,128)(2,1)S(1)}, bf16[272,384]{1,0:T(8,128)(2,1)}, u32[]{:S(2)}) copy-start(bf16[272,384]{1,0:T(8,128)(2,1)} %copy-done.21) | copy-start | bytes 626692
  162.3 38.9 %copy-start.11 = (bf16[1,256,384]{2,1,0:T(8,128)(2,1)S(1)}, bf16[1,256,384]{2,1,0:T(8,128)(2,1)}, u32[]{:S(2)}) copy-start(bf16[1,256,384]{2,1,0:T(8,128)(2,1)} %param.11) | copy-start | bytes 589828
  162.4 43.2 %copy-start.14 = (bf16[1,256,384]{2,1,0:T(8,128)(2,1)S(1)}, bf16[1,256,384]{2,1,0:T(8,128)(2,1)}, u32[]{:S(2)}) copy-start(bf16[1,256,384]{2,1,0:T(8,128)(2,1)} %param.12) | copy-start | bytes 589828
  164.0 15.0 %collective-permute-start.25 = (f32[4,256]{1,0:T(4,128)S(1)}, f32[4,256]{1,0:T(4,128)S(1)}, u32[]{:S(2)}, u32[]{:S(2)}) collective-permute-start(f32[4,256]{1,0:T(4,128)S(1)} %pad_maximum_fusion.5), channel_id=1, source_target_pairs={{0,3},{1,0},{2,1},{3,2},{4,7},{5,4},{6,5},{7,6},{8,11},{9,8},{10,9... | collective-permute-start | bytes 12296 | tf_op jit(solution)/shard_map/ppermute | solution.py:18
  165.4 18.8 %collective-permute-start.24 = (f32[4,256]{1,0:T(4,128)S(1)}, f32[4,256]{1,0:T(4,128)S(1)}, u32[]{:S(2)}, u32[]{:S(2)}) collective-permute-start(f32[4,256]{1,0:T(4,128)S(1)} %pad_maximum_fusion.5), channel_id=1, source_target_pairs={{0,1},{1,2},{2,3},{3,0},{4,5},{5,6},{6,7},{7,4},{8,9},{9,10},{10,1... | collective-permute-start | bytes 12296 | tf_op jit(solution)/shard_map/ppermute | solution.py:18
  167.6 16.6 %collective-permute-start.23 = (f32[4,256]{1,0:T(4,128)S(1)}, f32[4,256]{1,0:T(4,128)S(1)}, u32[]{:S(2)}, u32[]{:S(2)}) collective-permute-start(f32[4,256]{1,0:T(4,128)S(1)} %pad_maximum_fusion.5), channel_id=1, source_target_pairs={{0,2},{1,3},{2,0},{3,1},{4,6},{5,7},{6,4},{7,5},{8,10},{9,11},{10,... | collective-permute-start | bytes 12296 | tf_op jit(solution)/shard_map/ppermute | solution.py:18
  170.6 13.6 %collective-permute-start.26 = (bf16[256,384]{1,0:T(8,128)(2,1)S(1)}, bf16[256,384]{1,0:T(8,128)(2,1)S(1)}, u32[]{:S(2)}, u32[]{:S(2)}) collective-permute-start(bf16[256,384]{1,0:T(8,128)(2,1)S(1)} %get-tuple-element.127), channel_id=1, source_target_pairs={{0,17},{1,18},{2,19},{3,16},{16,33},{17,34},{18,35},{19,32},{32,49... | collective-permute-start | bytes 589832 | tf_op jit(solution)/shard_map/ppermute | solution.py:34
  174.3 16.6 %collective-permute-start.27 = (bf16[256,384]{1,0:T(8,128)(2,1)S(1)}, bf16[256,384]{1,0:T(8,128)(2,1)S(1)}, u32[]{:S(2)}, u32[]{:S(2)}) collective-permute-start(bf16[256,384]{1,0:T(8,128)(2,1)S(1)} %get-tuple-element.115), channel_id=1, source_target_pairs={{0,18},{1,19},{2,16},{3,17},{16,34},{17,35},{18,32},{19,33},{32,50... | collective-permute-start | bytes 589832 | tf_op jit(solution)/shard_map/ppermute | solution.py:34
  179.0 16.1 %collective-permute-start.28 = (bf16[256,384]{1,0:T(8,128)(2,1)S(1)}, bf16[256,384]{1,0:T(8,128)(2,1)S(1)}, u32[]{:S(2)}, u32[]{:S(2)}) collective-permute-start(bf16[256,384]{1,0:T(8,128)(2,1)S(1)} %get-tuple-element.126), channel_id=1, source_target_pairs={{0,19},{1,16},{2,17},{3,18},{16,35},{17,32},{18,33},{19,34},{32,51... | collective-permute-start | bytes 589832 | tf_op jit(solution)/shard_map/ppermute | solution.py:34
  195.2 10.4 %collective-permute-start.31 = (f32[4,256]{1,0:T(4,128)S(1)}, f32[4,256]{1,0:T(4,128)S(1)}, u32[]{:S(2)}, u32[]{:S(2)}) collective-permute-start(f32[4,256]{1,0:T(4,128)S(1)} %add_add_fusion), channel_id=1, source_target_pairs={{0,12},{4,0},{8,4},{12,8},{1,13},{5,1},{9,5},{13,9},{2,14},{6,2},{... | collective-permute-start | bytes 12296 | tf_op jit(solution)/shard_map/ppermute | solution.py:18
  198.1 7.5 %collective-permute-start.30 = (f32[4,256]{1,0:T(4,128)S(1)}, f32[4,256]{1,0:T(4,128)S(1)}, u32[]{:S(2)}, u32[]{:S(2)}) collective-permute-start(f32[4,256]{1,0:T(4,128)S(1)} %add_add_fusion), channel_id=1, source_target_pairs={{0,4},{4,8},{8,12},{12,0},{1,5},{5,9},{9,13},{13,1},{2,6},{6,10},{... | collective-permute-start | bytes 12296 | tf_op jit(solution)/shard_map/ppermute | solution.py:18
  198.1 7.5 %collective-permute-start.29 = (f32[4,256]{1,0:T(4,128)S(1)}, f32[4,256]{1,0:T(4,128)S(1)}, u32[]{:S(2)}, u32[]{:S(2)}) collective-permute-start(f32[4,256]{1,0:T(4,128)S(1)} %add_add_fusion), channel_id=1, source_target_pairs={{0,8},{4,12},{8,0},{12,4},{1,9},{5,13},{9,1},{13,5},{2,10},{6,14},... | collective-permute-start | bytes 12296 | tf_op jit(solution)/shard_map/ppermute | solution.py:18
  201.3 6.9 %collective-permute-start.22 = (bf16[256,384]{1,0:T(8,128)(2,1)S(1)}, bf16[256,384]{1,0:T(8,128)(2,1)S(1)}, u32[]{:S(2)}, u32[]{:S(2)}) collective-permute-start(bf16[256,384]{1,0:T(8,128)(2,1)S(1)} %fusion.4), channel_id=1, source_target_pairs={{0,16},{1,17},{2,18},{3,19},{16,32},{17,33},{18,34},{19,35},{32,48... | collective-permute-start | bytes 589832 | tf_op jit(solution)/shard_map/ppermute | solution.py:34
  205.8 7.0 %collective-permute-start.32 = (bf16[256,384]{1,0:T(8,128)(2,1)S(1)}, bf16[256,384]{1,0:T(8,128)(2,1)S(1)}, u32[]{:S(2)}, u32[]{:S(2)}) collective-permute-start(bf16[256,384]{1,0:T(8,128)(2,1)S(1)} %fusion), channel_id=1, source_target_pairs={{16,0},{32,16},{48,32},{64,48},{80,64},{96,80},{112,96},{128,112},... | collective-permute-start | bytes 589832 | tf_op jit(solution)/shard_map/ppermute | solution.py:24
